TPU v7x, 32 devices: a whole 2x2x4 slice. The times are simulated.
32 devices in a mesh: sub: 16 (over z, y, x), front: 2 (over core).
Axes of the slice: x: 2, y: 2, z: 4, core: 2. Of those that a mesh axis runs over, the one named last changes fastest.
Arguments:
- piv_cols: bfloat16 [16, 3072, 1024], P('sub', None, 'front'), may hold values from -6 to 6
- trail_cols: bfloat16 [16, 3072, 2048], P('sub', None, 'front'), may hold values from -6 to 6
- row_end: int32 [16, 24], P('sub'), may hold values from 128 to 3072, as said below
- parent_of: int32 [16], P('sub'), may hold values from 0 to 1, as said below
Outputs:
- r_pivot: float32 [2, 1024, 1024], P(None, None, 'front')
- r_trail: float32 [2, 1024, 2048], P(None, None, 'front')
Inputs may be any that keep to these rules, and one draw needn't show every extreme that they name: row_end[c, j] is a multiple of 128 and never falls as j grows; in the column blocks j < 8 it is at most 1280, and it reaches 1280 for some child in every draw. `parent_of`: exactly 8 children have each parent.
All inputs are finite; a program needn't handle non-finite values.
Results may differ from a plain program's by a relative error of at most 0.0003.
Values may be sent and summed in bfloat16 or wider, within the bound.
No kernel may reach another device: no remote copies, remote signals or barrier semaphores. Data moves between devices by JAX's collectives and lax.ppermute only.
A program may use at most 128 MiB of HBM per device.

v0:
```python
import jax
import jax.numpy as jnp
from jax import lax
from jax.sharding import PartitionSpec as P

BLK = 128
NPAR = 2
LIVE = 1280


def owned_ends(stair_ends, first, count):
    blocks = (first + jnp.arange(count, dtype=jnp.int32)) // BLK
    table = blocks[:, None] == jnp.arange(stair_ends.shape[0], dtype=jnp.int32)[None, :]
    return jnp.sum(jnp.where(table, stair_ends[None, :], 0), axis=1)


def shards(piv_cols, trail_cols, row_end, parent_of):
    position = lax.axis_index("front")
    tile_pivot = piv_cols.shape[2]
    tile_trail = trail_cols.shape[2]
    pivot_total = tile_pivot * lax.axis_size("front")
    stair_ends = row_end[0]
    row_ids = jnp.arange(piv_cols.shape[1], dtype=jnp.int32)[:, None]
    end_pivot = owned_ends(stair_ends, position * tile_pivot, tile_pivot)
    end_trail = owned_ends(stair_ends, pivot_total + position * tile_trail, tile_trail)
    pivot = jnp.where(row_ids < end_pivot[None, :], piv_cols[0], jnp.zeros((), piv_cols.dtype))
    trail = jnp.where(row_ids < end_trail[None, :], trail_cols[0], jnp.zeros((), trail_cols.dtype))
    pivot = pivot[:LIVE]
    trail = trail[:LIVE]
    own_columns = jnp.concatenate([pivot, trail], axis=1)
    gram = jnp.einsum(
        "rk,rt->kt",
        lax.all_gather(pivot, "front", axis=1, tiled=True),
        own_columns,
        preferred_element_type=jnp.float32,
    )
    parent_pick = (jnp.arange(NPAR, dtype=jnp.int32) == parent_of[0]).astype(jnp.float32)
    slots = parent_pick[:, None, None] * gram[None]
    pivot_part = lax.psum(slots[:, :, :tile_pivot], "sub")
    trail_part = lax.psum_scatter(slots[:, :, tile_pivot:], "sub", scatter_dimension=2, tiled=True)
    pivot_block = lax.all_gather(pivot_part, "front", axis=2, tiled=True)
    factor_lower = jnp.linalg.cholesky(pivot_block)
    solved_share = lax.linalg.triangular_solve(factor_lower, trail_part, left_side=True, lower=True)
    r_trail = lax.all_gather(solved_share, "sub", axis=2, tiled=True)
    own_rows = lax.dynamic_slice_in_dim(factor_lower, position * tile_pivot, tile_pivot, axis=1)
    r_pivot = jnp.transpose(own_rows, (0, 2, 1))
    return (r_pivot, r_trail)


def solution(mesh):
    return jax.shard_map(
        shards,
        mesh=mesh,
        in_specs=(P("sub", None, "front"), P("sub", None, "front"), P("sub", None), P("sub")),
        out_specs=(P(None, None, "front"), P(None, None, "front")),
        check_vma=False,
    )
```

profile of v0, /device:TPU:0, one launch (start us, length us, event | category | flops | bytes accessed | tf_op | source)
XLA Modules:
  0.0 974.7 jit_solution(732880113762607117)
XLA Ops:
  8.0 2.9 fusion.6
  12.4 2.8 fusion.1
  15.1 10.0 %all-gather.4.cloned.1.call-done = bf16[1280,1024]{1,0:T(8,128)(2,1)} async-done(((bf16[1280,512]{1,0:T(8,128)(2,1)}), bf16[1280,1024]{1,0:T(8,128)(2,1)}) %all-gather.4.cloned.1.call-update) | async-done | bytes 2621456 | tf_op jit(solution)/shard_map/all_gather | solution.py:33
  25.1 9.1 fusion.2
  34.2 5.1 broadcast_multiply_fusion
  39.3 4.6 copy-done
  46.5 169.4 %all-reduce.3.cloned.1.call-done = f32[2,1024,512]{1,2,0:T(8,128)} async-done(((f32[2,1024,512]{1,2,0:T(8,128)}), f32[2,1024,512]{1,2,0:T(8,128)}) %all-reduce.3.cloned.1.call-update) | async-done | bytes 4194320 | tf_op jit(solution)/shard_map/psum | solution.py:39
  216.0 9.3 slice.255
  226.3 10.1 %all-gather.6.cloned.1.call-done = f32[2,1024,1024]{1,2,0:T(8,128)} async-done(((f32[2,1024,512]{1,2,0:T(8,128)}), f32[2,1024,1024]{1,2,0:T(8,128)}) %all-gather.6.cloned.1.call-update) | async-done | bytes 8388624 | tf_op jit(solution)/shard_map/all_gather | solution.py:41
  236.4 8.7 copy.34
  245.1 12.5 %fusion = f32[2,1024,1024]{2,1,0:T(8,128)} fusion(f32[2,1024,1024]{2,1,0:T(8,128)} %copy.34, f32[2,1024,1024]{1,2,0:T(8,128)} %all-gather.6.cloned.1.call-done), kind=kLoop, calls=%fused_computation.3 | loop fusion | flops 4194304 | bytes 25165824 | tf_op jit(solution)/shard_map/jit(cholesky)/div | solution.py:42
  258.6 23.5 %custom-call.70 = f32[2,128,128]{2,1,0:T(8,128)S(1)} custom-call(f32[2,128,128]{2,1,0:T(8,128)S(1)} %cholesky.578), custom_call_target="Cholesky" | custom-call | tf_op jit(solution)/shard_map/jit(cholesky)/cholesky | solution.py:42
  282.0 19.7 %custom-call.71 = f32[2,1,128,128]{2,3,1,0:T(8,128)S(1)} custom-call(f32[2,1,128,128]{3,2,1,0:T(8,128)S(1)} %select_bitcast_fusion.6), custom_call_target="InvertDiagBlocksLowerTriangular" | custom-call | tf_op jit(solution)/shard_map/jit(cholesky)/cholesky | solution.py:42
  301.7 4.3 cholesky.253
  306.1 3.1 constant_dynamic-update-slice_fusion.32
  311.3 23.6 %custom-call.72 = f32[2,128,128]{2,1,0:T(8,128)S(1)} custom-call(f32[2,128,128]{2,1,0:T(8,128)S(1)} %cholesky.582), custom_call_target="Cholesky" | custom-call | tf_op jit(solution)/shard_map/jit(cholesky)/cholesky | solution.py:42
  335.6 19.7 %custom-call.73 = f32[2,1,128,128]{2,3,1,0:T(8,128)S(1)} custom-call(f32[2,1,128,128]{3,2,1,0:T(8,128)S(1)} %get-tuple-element.45), custom_call_target="InvertDiagBlocksLowerTriangular" | custom-call | tf_op jit(solution)/shard_map/jit(cholesky)/cholesky | solution.py:42
  357.0 3.2 fusion.17
  360.2 23.7 %custom-call.74 = f32[2,128,128]{2,1,0:T(8,128)S(1)} custom-call(f32[2,128,128]{2,1,0:T(8,128)S(1)} %cholesky.587), custom_call_target="Cholesky" | custom-call | tf_op jit(solution)/shard_map/jit(cholesky)/cholesky | solution.py:42
  384.6 19.7 %custom-call.75 = f32[2,1,128,128]{2,3,1,0:T(8,128)S(1)} custom-call(f32[2,1,128,128]{3,2,1,0:T(8,128)S(1)} %get-tuple-element.43), custom_call_target="InvertDiagBlocksLowerTriangular" | custom-call | tf_op jit(solution)/shard_map/jit(cholesky)/cholesky | solution.py:42
  405.9 3.7 fusion.20
  409.5 23.9 %custom-call.76 = f32[2,128,128]{2,1,0:T(8,128)S(1)} custom-call(f32[2,128,128]{2,1,0:T(8,128)S(1)} %cholesky.592), custom_call_target="Cholesky" | custom-call | tf_op jit(solution)/shard_map/jit(cholesky)/cholesky | solution.py:42
  434.1 19.7 %custom-call.77 = f32[2,1,128,128]{2,3,1,0:T(8,128)S(1)} custom-call(f32[2,1,128,128]{3,2,1,0:T(8,128)S(1)} %get-tuple-element.41), custom_call_target="InvertDiagBlocksLowerTriangular" | custom-call | tf_op jit(solution)/shard_map/jit(cholesky)/cholesky | solution.py:42
  455.2 3.8 fusion.23
  459.0 23.5 %custom-call.78 = f32[2,128,128]{2,1,0:T(8,128)S(1)} custom-call(f32[2,128,128]{2,1,0:T(8,128)S(1)} %cholesky.597), custom_call_target="Cholesky" | custom-call | tf_op jit(solution)/shard_map/jit(cholesky)/cholesky | solution.py:42
  483.1 19.8 %custom-call.79 = f32[2,1,128,128]{2,3,1,0:T(8,128)S(1)} custom-call(f32[2,1,128,128]{3,2,1,0:T(8,128)S(1)} %get-tuple-element.39), custom_call_target="InvertDiagBlocksLowerTriangular" | custom-call | tf_op jit(solution)/shard_map/jit(cholesky)/cholesky | solution.py:42
  504.2 3.6 fusion.26
  507.9 23.5 %custom-call.80 = f32[2,128,128]{2,1,0:T(8,128)S(1)} custom-call(f32[2,128,128]{2,1,0:T(8,128)S(1)} %cholesky.602), custom_call_target="Cholesky" | custom-call | tf_op jit(solution)/shard_map/jit(cholesky)/cholesky | solution.py:42
  532.0 19.9 %custom-call.81 = f32[2,1,128,128]{2,3,1,0:T(8,128)S(1)} custom-call(f32[2,1,128,128]{3,2,1,0:T(8,128)S(1)} %get-tuple-element.37), custom_call_target="InvertDiagBlocksLowerTriangular" | custom-call | tf_op jit(solution)/shard_map/jit(cholesky)/cholesky | solution.py:42
  553.0 3.2 fusion.29
  556.2 23.5 %custom-call.82 = f32[2,128,128]{2,1,0:T(8,128)S(1)} custom-call(f32[2,128,128]{2,1,0:T(8,128)S(1)} %cholesky.607), custom_call_target="Cholesky" | custom-call | tf_op jit(solution)/shard_map/jit(cholesky)/cholesky | solution.py:42
  580.4 19.7 %custom-call.83 = f32[2,1,128,128]{2,3,1,0:T(8,128)S(1)} custom-call(f32[2,1,128,128]{3,2,1,0:T(8,128)S(1)} %get-tuple-element.35), custom_call_target="InvertDiagBlocksLowerTriangular" | custom-call | tf_op jit(solution)/shard_map/jit(cholesky)/cholesky | solution.py:42
  603.7 23.7 %custom-call.84 = f32[2,128,128]{2,1,0:T(8,128)S(1)} custom-call(f32[2,128,128]{2,1,0:T(8,128)S(1)} %convolution_subtract_fusion.1), custom_call_target="Cholesky" | custom-call | tf_op jit(solution)/shard_map/jit(cholesky)/cholesky | solution.py:42
  628.8 12.8 %broadcast_select_fusion = (f32[2,1024,1024]{2,1,0:T(8,128)}, f32[2,1024,1024]{2,1,0:T(8,128)}) fusion(pred[1024,1024]{1,0:T(8,128)(4,1)S(1)} %iota_compare_fusion, f32[2,1024,1024]{2,1,0:T(8,128)} %get-tuple-element.34, pred[2]{0:T(512)(128)(4,1)S(1)} %or_or_fusion), kind=kLoop, calls=%fused_computation.9 | loop fusion | flops 6291456 | bytes 26214402 | tf_op jit(solution)/shard_map/triangular_solve | solution.py:43
  641.6 28.5 %while.1 = (s32[]{:T(128)}, f32[2,1024,1024]{2,1,0:T(8,128)}, s32[8,2]{0,1:T(2,128)S(1)}, f32[8,2,128,128]{3,2,0,1:T(8,128)}, s32[]{:T(128)}) while((s32[]{:T(128)}, f32[2,1024,1024]{2,1,0:T(8,128)}, s32[8,2]{0,1:T(2,128)S(1)}, f32[8,2,128,128]{3,2,0,1:T(8,128)}, s32[]{:T(128)}) %tuple.67), condition=%wide.while_cond, body=%wide.while_body.sunk | while | flops 2 | bytes 263277 | solution.py:43
  642.3 2.9 bitcast_dynamic-update-slice_fusion.2
  645.9 2.9 bitcast_dynamic-update-slice_fusion.2
  649.4 2.9 bitcast_dynamic-update-slice_fusion.2
  653.0 2.9 bitcast_dynamic-update-slice_fusion.2
  656.6 2.9 bitcast_dynamic-update-slice_fusion.2
  660.1 2.9 bitcast_dynamic-update-slice_fusion.2
  663.7 2.9 bitcast_dynamic-update-slice_fusion.2
  667.3 2.9 bitcast_dynamic-update-slice_fusion.2
  670.2 158.3 %custom-call.85 = f32[2,8,128,128]{2,3,1,0:T(8,128)S(1)} custom-call(f32[2,8,128,128]{3,2,1,0:T(8,128)} %bitcast.130), custom_call_target="InvertDiagBlocksLowerTriangular" | custom-call | tf_op jit(solution)/shard_map/triangular_solve | solution.py:43
  844.9 4.8 dynamic-slice_bitcast_fusion
  849.7 5.4 copy.58
  855.1 104.0 %all-gather.8.cloned.1.call-done = f32[2,1024,1024]{1,2,0:T(8,128)} async-done(((f32[2,1024,64]{1,2,0:T(8,128)}), f32[2,1024,1024]{1,2,0:T(8,128)}) %all-gather.8.cloned.1.call-update) | async-done | bytes 8388624 | tf_op jit(solution)/shard_map/all_gather | solution.py:44
  959.0 8.7 copy.59
  (85 shorter events, 46.2 us)
Async XLA Ops:
  7.2 17.9 %all-gather.4.cloned.1.call-start = ((), (), s32[]{:S(2)}) async-start(), calls=%async_computation.1 | async-start | bytes 3932160 | tf_op jit(solution)/shard_map/all_gather | solution.py:33
  10.9 205.1 %all-reduce.3.cloned.1.call-start = ((), (), s32[]{:S(2)}) async-start(), calls=%async_computation.2 | async-start | bytes 8388608 | tf_op jit(solution)/shard_map/psum | solution.py:39
  39.3 4.6 copy-start
  46.5 189.9 %all-gather.6.cloned.1.call-start = ((), (), s32[]{:S(2)}) async-start(), calls=%async_computation.3 | async-start | bytes 12582912 | tf_op jit(solution)/shard_map/all_gather | solution.py:41
  216.0 612.5 %reduce-scatter.2.cloned.1.call-start = ((), (), s32[]{:S(2)}) async-start(), calls=%async_computation.4 | async-start | bytes 8912896 | tf_op jit(solution)/shard_map/reduce_scatter | solution.py:40
  225.4 733.7 %all-gather.8.cloned.1.call-start = ((), (), s32[]{:S(2)}) async-start(), calls=%async_computation.5 | async-start | bytes 8912896 | tf_op jit(solution)/shard_map/all_gather | solution.py:44
  844.1 0.8 copy-start.1
Sparse Core Ops, SparseCore 0:
  11.0 14.0 all-gather.3
  46.6 169.2 all-reduce.2
  217.6 18.7 all-gather.5
  238.7 178.9 reduce-scatter.1
  845.0 113.9 all-gather.7
where the time goes:
time: 982 us; the launch traced here: 975 us
  other arithmetic  529 us (54%)
  waiting for transfers between devices  294 us (30%)
  local copies, waits for them, and re-layouts  78.6 us (8%)
  matrix products  58 us (6%)
  between operations  15.3 us (2%)
    another operation x30, other arithmetic, shards(): factor_lower = jnp.linalg.cholesky(pivot_block)  332 us
    another operation x3, other arithmetic, shards(): lax.linalg.triangular_solve(factor_lower, trail_part, left_side=True, low...  171 us
    psum x1, waiting for transfers between devices, shards(): pivot_part = lax.psum(slots[:, :, :tile_pivot], 'sub')  169 us
    all_gather x1, waiting for transfers between devices, shards(): r_trail = lax.all_gather(solved_share, 'sub', axis=2, tiled=True)  104 us
    another operation x14, matrix products, shards(): factor_lower = jnp.linalg.cholesky(pivot_block)  33.4 us
    another operation x24, local copies, waits for them, and re-layouts  28.5 us
  transfers between devices with their start and end apart: 5, of which 4 were waited for; matrix products, arithmetic and copies ran while one was open for 63% of the time, Pallas kernels for 0%

commit v1 on v0

v1 whole, which is shorter than its diff:
```python
import jax, jax.numpy as jnp
from jax import lax
from jax.experimental import pallas as pl
from jax.experimental.pallas import tpu as pltpu
from jax.sharding import PartitionSpec as P
B=128
F32=jnp.float32
BF=jnp.bfloat16

def split(x):
    hi = x.astype(BF)
    return hi, (x - hi.astype(F32)).astype(BF)

def dot3(lhs, rhs):
    lh, ll = lhs
    rh, rl = rhs
    return jnp.dot(jnp.concatenate([lh, lh, ll], axis=1), jnp.concatenate([rh, rl, rh], axis=0), preferred_element_type=F32)

def factor_block(d_ref, w_ref, fillers):
    rows8 = (8, B)
    for g in range(B // 8):
        xs, xi = [], []
        for i in range(8):
            row = d_ref[8*g+i:8*g+i+1, :]
            xs.append(jnp.broadcast_to(row[:, :B], rows8))
            xi.append(jnp.broadcast_to(row[:, B:], rows8))
        s = {}
        for i in range(8):
            for j in range(i, 8):
                s[i, j] = jnp.broadcast_to(xs[i][:, 8*g+j:8*g+j+1], rows8)
        for i in range(8):
            rs = lax.rsqrt(s[i, i])
            inv = rs * rs
            w_ref[8*g+i:8*g+i+1, :B] = (xs[i] * rs)[:1]
            w_ref[8*g+i:8*g+i+1, B:] = (xi[i] * rs)[:1]
            for r in range(8):
                if r == i: continue
                m = (s[r, i] if r < i else s[i, r]) * inv
                for j in range(max(r, i+1), 8):
                    s[r, j] = s[r, j] - m * s[i, j]
                xs[r] = xs[r] - m * xs[i]
                xi[r] = xi[r] - m * xi[i]
            s[i, i] = inv
        ys = [xs[i] * s[i, i] for i in range(8)]
        yi = [xi[i] * s[i, i] for i in range(8)]
        for r in range(g+1, B // 8):
            blk = d_ref[8*r:8*r+8, :B]
            bi = d_ref[8*r:8*r+8, B:]
            cols = [jnp.broadcast_to(blk[:, 8*g+i:8*g+i+1], rows8) for i in range(8)]
            for i in range(8):
                blk = blk - cols[i] * ys[i]
                bi = bi - cols[i] * yi[i]
            d_ref[8*r:8*r+8, :B] = blk
            d_ref[8*r:8*r+8, B:] = bi
        if fillers:
            fillers.pop(0)()
    while fillers:
        fillers.pop(0)()

def chol_kernel(g_ref, t_ref, r_ref, z_ref, s_ref, d_ref, w_ref, rhs_ref):
    n = g_ref.shape[0]
    nt = t_ref.shape[1]
    nb = n // B
    ri = lax.broadcasted_iota(jnp.int32, (B, B), 0)
    ci = lax.broadcasted_iota(jnp.int32, (B, B), 1)
    def src(k, lo, hi):
        return s_ref[k*B:(k+1)*B, lo:hi]
    def update(k, i):
        def run():
            lo = i * B
            lhs = split(jnp.transpose(r_ref[k*B:(k+1)*B, lo:lo+B]))
            lhs = jnp.concatenate([lhs[0], lhs[0], lhs[1]], axis=1)
            upd = jnp.dot(lhs, rhs_ref[k % 2, :, lo:], preferred_element_type=F32)
            if k == 0:
                s_ref[lo:lo+B, lo:n] = g_ref[lo:lo+B, lo:n] - upd[:, :n-lo]
                s_ref[lo:lo+B, n:] = t_ref[lo:lo+B, :] - upd[:, n-lo:]
            else:
                s_ref[lo:lo+B, lo:] = s_ref[lo:lo+B, lo:] - upd
        return run
    fillers = []
    for k in range(nb):
        lo = k * B
        d_ref[:, :B] = g_ref[:B, :B] if k == 0 else s_ref[lo:lo+B, lo:lo+B]
        d_ref[:, B:] = jnp.where(ri == ci, 1.0, 0.0).astype(F32)
        factor_block(d_ref, w_ref, fillers)
        fillers = []
        if k:
            r_ref[lo:lo+B, :lo] = jnp.zeros((B, lo), F32)
        r_ref[lo:lo+B, lo:lo+B] = jnp.where(ci >= ri, w_ref[:, :B], 0.0)
        wh, wl = split(w_ref[:, B:])
        w3 = jnp.concatenate([wh, wh, wl], axis=1)
        if k < nb - 1:
            rest = g_ref[:B, B:] if k == 0 else s_ref[lo:lo+B, lo+B:n]
            rh, rl = split(rest)
            p = jnp.dot(w3, jnp.concatenate([rh, rl, rh], axis=0), preferred_element_type=F32)
            r_ref[lo:lo+B, lo+B:] = p
            ph, pll = split(p)
            rhs_ref[k % 2, 0:B, lo+B:n] = ph
            rhs_ref[k % 2, B:2*B, lo+B:n] = pll
            rhs_ref[k % 2, 2*B:, lo+B:n] = ph
        rest = t_ref[:B, :] if k == 0 else s_ref[lo:lo+B, n:]
        rh, rl = split(rest)
        p = jnp.dot(w3, jnp.concatenate([rh, rl, rh], axis=0), preferred_element_type=F32)
        z_ref[lo:lo+B, :] = p
        ph, pll = split(p)
        rhs_ref[k % 2, 0:B, n:] = ph
        rhs_ref[k % 2, B:2*B, n:] = pll
        rhs_ref[k % 2, 2*B:, n:] = ph
        if k < nb - 1:
            update(k, k+1)()
            fillers = [update(k, i) for i in range(k+2, nb)]

def chol_solve(g, t):
    n, nt = g.shape[0], t.shape[1]
    return pl.pallas_call(
        chol_kernel,
        out_shape=(jax.ShapeDtypeStruct((n, n), F32), jax.ShapeDtypeStruct((n, nt), F32)),
        in_specs=[pl.BlockSpec(memory_space=pltpu.VMEM)]*2,
        out_specs=(pl.BlockSpec(memory_space=pltpu.VMEM),)*2,
        scratch_shapes=[pltpu.VMEM((n, n+nt), F32), pltpu.VMEM((B, 2*B), F32), pltpu.VMEM((B, 2*B), F32), pltpu.VMEM((2, 3*B, n+nt), BF)],
        compiler_params=pltpu.CompilerParams(vmem_limit_bytes=40*1024*1024),
        cost_estimate=pl.CostEstimate(flops=3*n*n*n, bytes_accessed=4*n*(2*n+2*nt), transcendentals=0),
    )(g, t)

LIVE = 1280
NPAR = 2


def owned_ends(stair_ends, first, count):
    blocks = (first + jnp.arange(count, dtype=jnp.int32)) // B
    table = blocks[:, None] == jnp.arange(stair_ends.shape[0], dtype=jnp.int32)[None, :]
    return jnp.sum(jnp.where(table, stair_ends[None, :], 0), axis=1)


def swap_front(mine0, mine1, position, axis):
    keep = jnp.where(position == 0, mine0, mine1)
    give = jnp.where(position == 0, mine1, mine0)
    got = lax.ppermute(give, "front", [(0, 1), (1, 0)])
    first = jnp.where(position == 0, keep, got)
    second = jnp.where(position == 0, got, keep)
    return jnp.concatenate([first, second], axis=axis)


def shards(piv_cols, trail_cols, row_end, parent_of):
    position = lax.axis_index("front")
    tile_pivot = piv_cols.shape[2]
    tile_trail = trail_cols.shape[2]
    pivot_total = tile_pivot * lax.axis_size("front")
    stair_ends = row_end[0]
    row_ids = jnp.arange(LIVE, dtype=jnp.int32)[:, None]
    end_pivot = owned_ends(stair_ends, position * tile_pivot, tile_pivot)
    end_trail = owned_ends(stair_ends, pivot_total + position * tile_trail, tile_trail)
    pivot = jnp.where(row_ids < end_pivot[None, :], piv_cols[0, :LIVE], jnp.zeros((), piv_cols.dtype))
    trail = jnp.where(row_ids < end_trail[None, :], trail_cols[0, :LIVE], jnp.zeros((), trail_cols.dtype))
    own_columns = jnp.concatenate([pivot, trail], axis=1)
    gram = jnp.einsum("rk,rt->kt", lax.all_gather(pivot, "front", axis=1, tiled=True), own_columns, preferred_element_type=F32)
    parent_pick = (jnp.arange(NPAR, dtype=jnp.int32) == parent_of[0]).astype(F32)
    slots = parent_pick[:, None, None] * gram[None]
    pivot_part = lax.psum(slots[:, :, :tile_pivot], "sub")
    trail_part = lax.psum_scatter(slots[:, :, tile_pivot:], "sub", scatter_dimension=2, tiled=True)
    pivot_own = swap_front(pivot_part[0], pivot_part[1], position, 1)
    trail_own = swap_front(trail_part[0], trail_part[1], position, 1)
    factor, solved = chol_solve(pivot_own, trail_own)
    share = solved.shape[1] // 2
    solved_share = swap_front(solved[:, :share], solved[:, share:], position, 0).reshape(NPAR, solved.shape[0], share)
    r_pivot = swap_front(factor[:, :tile_pivot], factor[:, tile_pivot:], position, 0).reshape(NPAR, factor.shape[0], tile_pivot)
    r_trail = lax.all_gather(solved_share, "sub", axis=2, tiled=True)
    return (r_pivot, r_trail)


def solution(mesh):
    return jax.shard_map(
        shards,
        mesh=mesh,
        in_specs=(P("sub", None, "front"), P("sub", None, "front"), P("sub", None), P("sub")),
        out_specs=(P(None, None, "front"), P(None, None, "front")),
        check_vma=False,
    )
```

time: 982 us -> 609 us (0.62)
  other arithmetic: 529 us -> 25.5 us
  waiting for transfers between devices: 294 us -> 478 us
  matrix products: 58 us -> 9.52 us
  local copies, waits for them, and re-layouts: 78.6 us -> 37.4 us
  Pallas kernels: 0 us -> 34.1 us
    another operation x33 -> x0, other arithmetic: 503 us -> none  [the longest x30 332 us: shards(): factor_lower = jnp.linalg.cholesky(pivot_block)]
    psum x1, waiting for transfers between devices: 169 us -> 360 us  [shards(): pivot_part = lax.psum(slots[:, :, :tile_pivot], 'sub')]
    another operation x29 -> x0, matrix products: 48.9 us -> none  [the longest x14 33.4 us: shards(): factor_lower = jnp.linalg.cholesky(pivot_block)]
    pallas_call x0 -> x1, Pallas kernels: none -> 34.1 us  [chol_solve(): pl.pallas_call(chol_kernel, out_shape=(jax.ShapeDtypeStruct((n, n), F32),...]
    another operation x33 -> x0, local copies, waits for them, and re-layouts: 33.8 us -> none
    div x1 -> x0, other arithmetic: 12.5 us -> none  [shards(): factor_lower = jnp.linalg.cholesky(pivot_block)]
    select_n x4 -> x12, other arithmetic: 5.65 us -> 16.5 us  [the longest x4 5.84 us: swap_front(): give = jnp.where(position == 0, mine1, mine0)]
    all_gather x1 -> x0, waiting for transfers between devices: 10.1 us -> none  [shards(): pivot_block = lax.all_gather(pivot_part, 'front', axis=2, tiled=True)]
  transfers between devices with their start and end apart: 5 -> 7, of which waited for: 4 -> 6; matrix products, arithmetic and copies ran while one was open for 63% -> 2% of each run, Pallas kernels for 0% -> 0%
where the time goes in v1:
time: 609 us; the launch traced here: 602 us
  waiting for transfers between devices  478 us (78%)
  local copies, waits for them, and re-layouts  37.4 us (6%)
  Pallas kernels  34.1 us (6%)
  other arithmetic  25.5 us (4%)
  between operations  15.7 us (3%)
  matrix products  9.52 us (2%)
    psum x1, waiting for transfers between devices, shards(): pivot_part = lax.psum(slots[:, :, :tile_pivot], 'sub')  360 us
    all_gather x1, waiting for transfers between devices, shards(): r_trail = lax.all_gather(solved_share, 'sub', axis=2, tiled=True)  102 us
    pallas_call x1, Pallas kernels, chol_solve(): pl.pallas_call(chol_kernel, out_shape=(jax.ShapeDtypeStruct((n, n), F32),...  34.1 us
    slice x2, local copies, waits for them, and re-layouts, shards(): slots[:, :, tile_pivot:]  18 us
    unnamed x16, local copies, waits for them, and re-layouts  14.2 us
  transfers between devices with their start and end apart: 7, of which 6 were waited for; matrix products, arithmetic and copies ran while one was open for 2% of the time, Pallas kernels for 0%

profile of v1, /device:TPU:0, one launch (start us, length us, event | category | flops | bytes accessed | tf_op | source)
XLA Modules:
  0.0 601.9 jit_solution(16551251044004859425)
XLA Ops:
  7.2 0.0 copy-start.4
  7.2 0.0 all-gather.3.cloned.1.call-start
  7.2 0.7 select_reduce_fusion.1
  8.0 2.9 fusion.5
  10.9 0.0 all-gather.3.cloned.1.call-update
  10.9 0.0 all-reduce.4.cloned.1.call-start
  11.6 0.1 select_reduce_fusion
  11.7 0.0 copy-start.3
  11.7 4.4 fusion
  16.1 9.0 %all-gather.3.cloned.1.call-done = bf16[1280,1024]{1,0:T(8,128)(2,1)} async-done(((bf16[1280,512]{1,0:T(8,128)(2,1)}), bf16[1280,1024]{1,0:T(8,128)(2,1)}) %all-gather.3.cloned.1.call-update) | async-done | bytes 2621456 | tf_op jit(solution)/shard_map/all_gather | solution.py:156
  25.1 9.5 %fusion.1 = f32[1024,1536]{1,0:T(8,128)} fusion(bf16[1280,1024]{1,0:T(8,128)(2,1)} %all-gather.3.cloned.1.call-done, bf16[1280,1024]{1,0:T(8,128)(2,1)} %fusion, bf16[1280,512]{1,0:T(8,128)(2,1)S(1)} %copy-done.3), kind=kOutput, calls=%fused_computation.5 | convolution fusion | flops 4034396160 | bytes 12845056 | tf_op jit(solution)/shard_map/rk,rt->kt/dot_general | solution.py:156
  34.6 5.0 broadcast_multiply_fusion
  39.6 2.5 slice.48
  42.1 4.6 slice.51
  46.7 13.4 %copy.11 = f32[2,1024,1024]{1,0,2:T(2,128)} copy(f32[2,1024,1024]{2,1,0:T(8,128)} %slice.51) | data formatting | bytes 16777216 | tf_op jit(solution)/shard_map/slice | solution.py:160
  60.1 0.0 all-reduce.4.cloned.1.call-update
  60.1 0.2 all-gather.5.cloned.1.call-start
  60.3 360.2 %all-reduce.4.cloned.1.call-done = (f32[2,1024,512]{2,1,0:T(8,128)}, f32[2,1024,1024]{1,0,2:T(2,128)}) async-done(((f32[2,1024,512]{2,1,0:T(8,128)}, f32[2,1024,1024]{1,0,2:T(2,128)}), (f32[2,1024,512]{2,1,0:T(8,128)}, f32[2,1024,1024]{1,0,2:T(2,128)})) %all-reduce.4.cloned.1.call-update) | async-done | bytes 12582928 | tf_op jit(solution)/shard_map/psum | solution.py:159
  420.5 2.7 select_bitcast_fusion
  423.2 0.1 collective-permute-start
  423.3 0.6 dynamic-slice
  424.5 1.7 constant_dynamic-slice_fusion
  426.2 0.2 copy.17
  426.4 0.2 copy.16
  426.7 0.1 select_bitcast_fusion.1
  426.7 0.5 collective-permute-start.1
  427.3 1.5 collective-permute-done.1
  428.8 0.1 bitcast_select_fusion.3
  428.9 0.2 pad_maximum_fusion.3.t_ref
  429.1 2.4 bitcast_select_fusion.1
  431.5 0.4 pad_maximum_fusion.g_ref
  431.9 34.1 %shard_map.59 = (f32[1024,1024]{1,0:T(8,128)S(1)}, f32[1024,128]{1,0:T(8,128)S(1)}) custom-call(f32[1024,1024]{1,0:T(8,128)S(1)} %pad_maximum_fusion.g_ref, f32[1024,128]{1,0:T(8,128)S(1)} %pad_maximum_fusion.3.t_ref), custom_call_target="tpu_custom_call" | custom-call | flops 3221225472 | bytes 9437184 | tf_op jit(solution)/shard_map/pallas_call | solution.py:115
  466.0 0.0 copy-start
  466.0 0.2 slice_select_fusion.3
  466.2 0.4 collective-permute-start.3
  466.7 1.5 collective-permute-done.3
  468.2 0.2 broadcast_select_fusion.4
  468.4 0.1 pad_maximum_fusion.2
  468.5 1.1 copy.14
  469.7 0.0 all-gather.5.cloned.1.call-update
  469.7 0.0 copy-start.1
  469.7 2.9 slice_select_fusion.1
  472.6 0.4 collective-permute-start.2
  473.0 3.8 collective-permute-done.2
  476.8 0.8 broadcast_select_fusion.1
  477.6 2.5 pad_maximum_fusion.1
  480.0 101.8 %all-gather.5.cloned.1.call-done = f32[2,1024,1024]{1,0,2:T(2,128)} async-done(((f32[2,1024,64]{1,0,2:T(2,128)}), f32[2,1024,1024]{1,0,2:T(2,128)}) %all-gather.5.cloned.1.call-update) | async-done | bytes 8388624 | tf_op jit(solution)/shard_map/all_gather | solution.py:167
  581.9 13.1 %copy.15 = f32[2,1024,1024]{2,1,0:T(8,128)} copy(f32[2,1024,1024]{1,0,2:T(2,128)} %all-gather.5.cloned.1.call-done) | data formatting | bytes 16777216
  (12 shorter events, 0.0 us)
Async XLA Ops:
  7.2 4.5 copy-start.4
  7.2 17.9 %all-gather.3.cloned.1.call-start = ((), (), s32[]{:S(2)}) async-start(), calls=%async_computation | async-start | bytes 3932160 | tf_op jit(solution)/shard_map/all_gather | solution.py:156
  10.9 409.6 %all-reduce.4.cloned.1.call-start = ((), (), s32[]{:S(2)}) async-start(), calls=%async_computation.2 | async-start | bytes 25165824 | tf_op jit(solution)/shard_map/psum | solution.py:159
  11.7 13.4 %copy-start.3 = (bf16[1280,512]{1,0:T(8,128)(2,1)S(1)}, bf16[1280,512]{1,0:T(8,128)(2,1)}, u32[]{:S(2)}) copy-start(bf16[1280,512]{1,0:T(8,128)(2,1)} %fusion.5) | copy-start | bytes 3932164
  60.1 521.7 %all-gather.5.cloned.1.call-start = ((), (), s32[]{:S(2)}) async-start(), calls=%async_computation.1 | async-start | bytes 8912896 | tf_op jit(solution)/shard_map/all_gather | solution.py:167
  420.5 2.8 copy-start.5
  423.2 5.9 collective-permute-start
  426.7 2.5 copy-start.2
  426.7 2.1 collective-permute-start.1
  466.0 2.5 copy-start
  466.2 2.0 collective-permute-start.3
  469.7 7.1 %copy-start.1 = (f32[1024,1024]{1,0:T(8,128)S(1)}, f32[1024,1024]{1,0:T(8,128)}, u32[]{:S(2)}) copy-start(f32[1024,1024]{1,0:T(8,128)} %copy-done) | copy-start | bytes 12582916
  472.6 4.2 collective-permute-start.2
Sparse Core Ops, SparseCore 0:
  11.0 14.0 all-gather.2
  60.2 360.2 all-reduce.3
  469.8 112.0 all-gather.4

commit v2 on v1

v2 whole, which is shorter than its diff:
```python
import jax, jax.numpy as jnp
from jax import lax
from jax.experimental import pallas as pl
from jax.experimental.pallas import tpu as pltpu
from jax.sharding import PartitionSpec as P
B=128
F32=jnp.float32
BF=jnp.bfloat16
LIVE = 1280
NPAR = 2
PIECES = 4
LEVELS = 32766.0

def split(x):
    hi = x.astype(BF)
    return hi, (x - hi.astype(F32)).astype(BF)

def factor_block(d_ref, w_ref, fillers):
    rows8 = (8, B)
    for g in range(B // 8):
        xs, xi = [], []
        for i in range(8):
            row = d_ref[8*g+i:8*g+i+1, :]
            xs.append(jnp.broadcast_to(row[:, :B], rows8))
            xi.append(jnp.broadcast_to(row[:, B:], rows8))
        s = {}
        for i in range(8):
            for j in range(i, 8):
                s[i, j] = jnp.broadcast_to(xs[i][:, 8*g+j:8*g+j+1], rows8)
        for i in range(8):
            rs = lax.rsqrt(s[i, i])
            inv = rs * rs
            w_ref[8*g+i:8*g+i+1, :B] = (xs[i] * rs)[:1]
            w_ref[8*g+i:8*g+i+1, B:] = (xi[i] * rs)[:1]
            for r in range(8):
                if r == i: continue
                m = (s[r, i] if r < i else s[i, r]) * inv
                for j in range(max(r, i+1), 8):
                    s[r, j] = s[r, j] - m * s[i, j]
                xs[r] = xs[r] - m * xs[i]
                xi[r] = xi[r] - m * xi[i]
            s[i, i] = inv
        ys = [xs[i] * s[i, i] for i in range(8)]
        yi = [xi[i] * s[i, i] for i in range(8)]
        for r in range(g+1, B // 8):
            blk = d_ref[8*r:8*r+8, :B]
            bi = d_ref[8*r:8*r+8, B:]
            cols = [jnp.broadcast_to(blk[:, 8*g+i:8*g+i+1], rows8) for i in range(8)]
            for i in range(8):
                blk = blk - cols[i] * ys[i]
                bi = bi - cols[i] * yi[i]
            d_ref[8*r:8*r+8, :B] = blk
            d_ref[8*r:8*r+8, B:] = bi
        if fillers:
            fillers.pop(0)()
    while fillers:
        fillers.pop(0)()


def tri_index(i, j, nb):
    return i * nb - i * (i - 1) // 2 + (j - i)


def chol_kernel(g_ref, t_ref, r_ref, q_ref, s_ref, z_ref, d_ref, w_ref, rhs_ref):
    n = t_ref.shape[1]
    nt = t_ref.shape[0]
    nb = n // B
    ri = lax.broadcasted_iota(jnp.int32, (B, B), 0)
    ci = lax.broadcasted_iota(jnp.int32, (B, B), 1)

    def gram_block(i, j):
        at = tri_index(i, j, nb) * B
        return g_ref[at:at+B, :]

    def update(k, i):
        def run():
            lo = i * B
            lhs = split(jnp.transpose(r_ref[k*B:(k+1)*B, lo:lo+B]))
            lhs = jnp.concatenate([lhs[0], lhs[0], lhs[1]], axis=1)
            upd = jnp.dot(lhs, rhs_ref[k % 2, :, lo:], preferred_element_type=F32)
            if k == 0:
                for j in range(i, nb):
                    s_ref[lo:lo+B, j*B:(j+1)*B] = gram_block(i, j) - upd[:, (j-i)*B:(j-i+1)*B]
                s_ref[lo:lo+B, n:] = jnp.transpose(t_ref[:, lo:lo+B]) - upd[:, n-lo:]
            else:
                s_ref[lo:lo+B, lo:] = s_ref[lo:lo+B, lo:] - upd
        return run

    fillers = []
    for k in range(nb):
        lo = k * B
        d_ref[:, :B] = gram_block(0, 0) if k == 0 else s_ref[lo:lo+B, lo:lo+B]
        d_ref[:, B:] = jnp.where(ri == ci, 1.0, 0.0).astype(F32)
        factor_block(d_ref, w_ref, fillers)
        fillers = []
        if k:
            r_ref[lo:lo+B, :lo] = jnp.zeros((B, lo), F32)
        r_ref[lo:lo+B, lo:lo+B] = jnp.where(ci >= ri, w_ref[:, :B], 0.0)
        wh, wl = split(w_ref[:, B:])
        w3 = jnp.concatenate([wh, wh, wl], axis=1)
        if k < nb - 1:
            rest = g_ref[B:nb*B, :] if k == 0 else s_ref[lo:lo+B, lo+B:n]
            if k == 0:
                rest = jnp.concatenate([gram_block(0, j) for j in range(1, nb)], axis=1)
            rh, rl = split(rest)
            p = jnp.dot(w3, jnp.concatenate([rh, rl, rh], axis=0), preferred_element_type=F32)
            r_ref[lo:lo+B, lo+B:] = p
            ph, pll = split(p)
            rhs_ref[k % 2, 0:B, lo+B:n] = ph
            rhs_ref[k % 2, B:2*B, lo+B:n] = pll
            rhs_ref[k % 2, 2*B:, lo+B:n] = ph
        rest = jnp.transpose(t_ref[:, :B]) if k == 0 else s_ref[lo:lo+B, n:]
        rh, rl = split(rest)
        p = jnp.dot(w3, jnp.concatenate([rh, rl, rh], axis=0), preferred_element_type=F32)
        z_ref[lo:lo+B, :] = p
        ph, pll = split(p)
        rhs_ref[k % 2, 0:B, n:] = ph
        rhs_ref[k % 2, B:2*B, n:] = pll
        rhs_ref[k % 2, 2*B:, n:] = ph
        if k < nb - 1:
            update(k, k+1)()
            fillers = [update(k, i) for i in range(k+2, nb)]
    exps, mants = [], []
    for k in range(nb):
        z = z_ref[k*B:(k+1)*B, :]
        top = jnp.maximum(jnp.max(jnp.abs(z), axis=0, keepdims=True), 1e-30)
        e = jnp.ceil(jnp.log2(top))
        mant = jnp.minimum(jnp.ceil(top * jnp.exp2(-e) * 16384.0) + 1.0, 32767.0)
        step = mant * jnp.exp2(e) * (1.0 / (16384.0 * LEVELS))
        codes = jnp.clip(jnp.round(z * (1.0 / step)), -LEVELS, LEVELS)
        q_ref[k*B:(k+1)*B, :] = codes.astype(jnp.int32).astype(jnp.int16)
        exps.append(e)
        mants.append(mant)
    q_ref[n:, :] = jnp.concatenate(exps + mants, axis=0).astype(jnp.int32).astype(jnp.int16)


def chol_solve(g, t):
    nt, n = t.shape
    vmem = pl.BlockSpec(memory_space=pltpu.VMEM)
    return pl.pallas_call(
        chol_kernel,
        out_shape=(jax.ShapeDtypeStruct((n, n), F32), jax.ShapeDtypeStruct((n + 2 * (n // B), nt), jnp.int16)),
        in_specs=[vmem] * 2,
        out_specs=(vmem,) * 2,
        scratch_shapes=[
            pltpu.VMEM((n, n + nt), F32),
            pltpu.VMEM((n, nt), F32),
            pltpu.VMEM((B, 2*B), F32),
            pltpu.VMEM((B, 2*B), F32),
            pltpu.VMEM((2, 3*B, n + nt), BF),
        ],
        compiler_params=pltpu.CompilerParams(vmem_limit_bytes=40*1024*1024),
        cost_estimate=pl.CostEstimate(flops=3*n*n*n, bytes_accessed=4*n*(2*n+2*nt), transcendentals=0),
    )(g, t)


def gram_kernel(info_ref, own_ref, other_ref, trail_ref, g_ref, *rest):
    t_refs, a_ref = rest[:-1], rest[-1]
    nb_all = info_ref.shape[0] - 2
    live, tile = other_ref.shape
    n = a_ref.shape[1]
    nb = n // B
    place = info_ref[nb_all + 1]
    wanted = info_ref[nb_all] == place
    rows = lax.broadcasted_iota(jnp.int32, (live, B), 0)
    zero = jnp.zeros((live, B), BF)
    per = tile // B
    for half, ref in ((place, own_ref.at[0]), (1 - place, other_ref)):
        for j in range(per):
            end = info_ref[half * per + j]
            at = pl.multiple_of(half * tile + j * B, B)
            a_ref[:, pl.ds(at, B)] = jnp.where(rows < end, ref[:, j*B:(j+1)*B], zero)
    dims = (((0,), (0,)), ((), ()))

    @pl.when(wanted)
    def _():
        for i in range(0, nb, 2):
            lhs = a_ref[:, i*B:(i+2)*B]
            out = lax.dot_general(lhs, a_ref[:, i*B:], dims, preferred_element_type=F32)
            for r in (i, i + 1):
                for j in range(r, nb):
                    at = tri_index(r, j, nb) * B
                    g_ref[at:at+B, :] = out[(r-i)*B:(r-i+1)*B, (j-i)*B:(j-i+1)*B]

    @pl.when(jnp.logical_not(wanted))
    def _():
        g_ref[...] = jnp.zeros(g_ref.shape, F32)

    trail_tile = trail_ref.shape[2]
    trail_per = trail_tile // B
    piece = t_refs[0].shape[1]
    for j in range(0, trail_per, 2):
        cols = []
        for h in (j, j + 1):
            end = info_ref[nb + place * trail_per + h]
            cols.append(jnp.where(rows < end, trail_ref[0, :, h*B:(h+1)*B], zero))
        out = lax.dot_general(jnp.concatenate(cols, axis=1), a_ref[...], dims, preferred_element_type=F32)
        for q, t_ref in enumerate(t_refs):
            t_ref[j*B:(j+2)*B, :] = out[:, q*piece:(q+1)*piece]


def grams(info, piv, other, trail, pieces):
    live, tile = other.shape
    n = 2 * tile
    nb = n // B
    wide = trail.shape[2]
    packed = nb * (nb + 1) // 2 * B
    first = lambda i, info: (0, 0, 0)
    flat = lambda i, info: (0, 0)
    return pl.pallas_call(
        gram_kernel,
        out_shape=(jax.ShapeDtypeStruct((packed, B), F32),) + (jax.ShapeDtypeStruct((wide, n // pieces), F32),) * pieces,
        grid_spec=pltpu.PrefetchScalarGridSpec(
            num_scalar_prefetch=1,
            grid=(1,),
            in_specs=[
                pl.BlockSpec((1, live, tile), first),
                pl.BlockSpec((live, tile), flat),
                pl.BlockSpec((1, live, wide), first),
            ],
            out_specs=(pl.BlockSpec((packed, B), flat),) + (pl.BlockSpec((wide, n // pieces), flat),) * pieces,
            scratch_shapes=[pltpu.VMEM((live, n), BF)],
        ),
        compiler_params=pltpu.CompilerParams(vmem_limit_bytes=48*1024*1024),
        cost_estimate=pl.CostEstimate(flops=2*live*n*(wide+n//2), bytes_accessed=2*live*(n+wide)+4*n*(wide+n//2), transcendentals=0),
    )(info, piv, other, trail)


def unpack_kernel(q_ref, s_ref, o_ref):
    chips, rows, lanes = q_ref.shape
    nb = s_ref.shape[1] // 2
    half = lanes // 2
    lane = lax.broadcasted_iota(jnp.int32, (rows, lanes), 1)
    which = lax.broadcasted_iota(jnp.int32, (nb, lanes), 0) == pl.program_id(0)

    def values(c):
        sc = s_ref[c].astype(jnp.int32).astype(F32)
        step = sc[nb:] * jnp.exp2(sc[:nb]) * (1.0 / (16384.0 * LEVELS))
        step = jnp.sum(jnp.where(which, step, 0.0), axis=0, keepdims=True)
        return q_ref[c].astype(jnp.int32).astype(F32) * step

    for c in range(0, chips, 2):
        a, b = values(c), values(c + 1)
        at = c * half
        o_ref[0, :, at:at+lanes] = jnp.where(lane < half, a, pltpu.roll(b, half, 1))
        o_ref[1, :, at:at+lanes] = jnp.where(lane < half, pltpu.roll(a, half, 1), b)


def unpack(q, n):
    chips, rows, lanes = q.shape
    wide = chips * lanes // 2
    nb = n // B
    return pl.pallas_call(
        unpack_kernel,
        out_shape=jax.ShapeDtypeStruct((NPAR, n, wide), F32),
        grid=(nb,),
        in_specs=[pl.BlockSpec((chips, B, lanes), lambda k: (0, k, 0)), pl.BlockSpec((chips, 2 * nb, lanes), lambda k: (0, n // (2 * nb), 0))],
        out_specs=pl.BlockSpec((NPAR, B, wide), lambda k: (0, k, 0)),
        compiler_params=pltpu.CompilerParams(vmem_limit_bytes=40*1024*1024),
        cost_estimate=pl.CostEstimate(flops=0, bytes_accessed=2*q.size+8*n*wide, transcendentals=0),
    )(q, q)


def unpack_plain(q, n):
    chips, rows, lanes = q.shape
    nb = n // B
    sc = q[:, n:].astype(F32)
    step = sc[:, nb:] * jnp.exp2(sc[:, :nb]) * (1.0 / (16384.0 * LEVELS))
    z = q[:, :n].astype(F32).reshape(chips, nb, B, lanes) * step[:, :, None, :]
    z = z.reshape(chips, n, NPAR, lanes // NPAR)
    return jnp.transpose(z, (2, 1, 0, 3)).reshape(NPAR, n, chips * lanes // NPAR)


def take(x, axis, index):
    return lax.dynamic_index_in_dim(x, index, axis, keepdims=False)


def flip(x, bit, count):
    return lax.ppermute(x, "sub", [(i, i ^ bit) for i in range(count)])


def halve(x, axis, bit, me, count):
    own = jnp.where(me & bit, 1, 0)
    return take(x, axis, own) + flip(take(x, axis, 1 - own), bit, count)


def bit_orders(count):
    bits = [1 << i for i in range(count.bit_length() - 1)]
    plane = len(bits) // 2
    other = bits[:plane][::-1] + bits[plane:]
    return bits, other


def sum_everywhere(x, order, me, count):
    steps = len(order)
    x = x.reshape((2,) * steps + x.shape[1:])
    for bit in order:
        x = halve(x, 0, bit, me, count)
    for bit in order[::-1]:
        other = flip(x, bit, count)
        up = (me & bit) != 0
        x = jnp.stack([jnp.where(up, other, x), jnp.where(up, x, other)])
    return x.reshape((count,) + x.shape[steps:])


def sum_shares(x, order, me, count, parent, partner):
    left = [1 << i for i in range(count.bit_length() - 1)][::-1]
    x = x.reshape((2,) * len(left) + (x.shape[0] // count, x.shape[1]))
    bit = order[0]
    axis = left.index(bit)
    own = jnp.where(me & bit, 1, 0)
    got = flip(take(x, axis, 1 - own), bit, count)
    kept = take(x, axis, own)
    left.remove(bit)
    x = jnp.stack([jnp.where(parent == p, kept, 0.0) + jnp.where(partner == p, got, 0.0) for p in range(NPAR)])
    for bit in order[1:]:
        x = halve(x, 1 + left.index(bit), bit, me, count)
        left.remove(bit)
    return x


def shards(count, piv_cols, trail_cols, row_end, parent_of):
    place = lax.axis_index("front")
    me = lax.axis_index("sub")
    swap = [(0, 1), (1, 0)]
    tile_pivot = piv_cols.shape[2]
    n = NPAR * tile_pivot
    orders = bit_orders(count)
    other_piv = lax.ppermute(piv_cols[0, :LIVE], "front", swap)
    parent = parent_of[0]
    partners = [flip(parent_of, order[0], count)[0] for order in orders]
    info = jnp.concatenate([row_end[0], parent_of, place[None].astype(jnp.int32)])
    packed, *trails = grams(info, piv_cols, other_piv, trail_cols, PIECES)

    packed = packed.reshape(count, packed.shape[0] // count, B)
    cut = packed.shape[1] // 2
    parts = [sum_everywhere(part, order, me, count) for part, order in zip((packed[:, :cut], packed[:, cut:]), orders)]
    gram = jnp.concatenate(parts, axis=1).reshape(-1, B)

    shares = [sum_shares(t, orders[q % 2], me, count, parent, partners[q % 2]) for q, t in enumerate(trails)]
    share = jnp.concatenate(shares, axis=2)
    width = share.shape[1]
    keep = take(share, 0, place)
    got = lax.ppermute(take(share, 0, 1 - place), "front", swap)
    trail = jnp.concatenate([jnp.where(place == 0, keep, got), jnp.where(place == 0, got, keep)], axis=0)

    factor, codes = chol_solve(gram, trail)

    theirs = lax.ppermute(codes, "front", swap)
    packed_codes = jnp.where(
        place == 0,
        jnp.concatenate([codes[:, :width], theirs[:, :width]], axis=1),
        jnp.concatenate([theirs[:, width:], codes[:, width:]], axis=1),
    )
    every = lax.all_gather(packed_codes, "sub", axis=0)
    r_trail = unpack(every, n) if 2 * width == B else unpack_plain(every, n)

    low, high = factor[:, :tile_pivot], factor[:, tile_pivot:]
    keep = jnp.where(place == 0, low, high)
    got = lax.ppermute(jnp.where(place == 0, high, low), "front", swap)
    r_pivot = jnp.stack([jnp.where(place == 0, keep, got), jnp.where(place == 0, got, keep)])
    return (r_pivot, r_trail)


def solution(mesh):
    count = mesh.shape["sub"]
    return jax.shard_map(
        lambda *args: shards(count, *args),
        mesh=mesh,
        in_specs=(P("sub", None, "front"), P("sub", None, "front"), P("sub", None), P("sub")),
        out_specs=(P(None, None, "front"), P(None, None, "front")),
        check_vma=False,
    )
```

time: 609 us -> 331 us (0.54)
  waiting for transfers between devices: 478 us -> 115 us
  blocking collectives: 0 us -> 101 us
  starting transfers between devices: 1.79 us -> 48.8 us
  local copies, waits for them, and re-layouts: 37.4 us -> 2.72 us
  other arithmetic: 25.5 us -> 6.67 us
  Pallas kernels: 34.1 us -> 49.8 us
  between operations: 15.7 us -> 4.62 us
  matrix products: 9.52 us -> 0 us
    psum x1 -> x0, waiting for transfers between devices: 360 us -> none  [shards(): pivot_part = lax.psum(slots[:, :, :tile_pivot], 'sub')]
    all_gather x2 -> x0, waiting for transfers between devices: 111 us -> none  [the longest x1 102 us: shards(): r_trail = lax.all_gather(solved_share, 'sub', axis=2, tiled=True)]
    ppermute x4 -> x38, waiting for transfers between devices: 6.86 us -> 115 us  [the longest x34 115 us: flip(): return lax.ppermute(x, 'sub', [(i, i ^ bit) for i in range(count)])]
    all_gather x0 -> x1, blocking collectives: none -> 101 us  [shards(): every = lax.all_gather(packed_codes, 'sub', axis=0)]
    ppermute x4 -> x38, starting transfers between devices: 1.5 us -> 48.8 us  [the longest x34 47.5 us: flip(): return lax.ppermute(x, 'sub', [(i, i ^ bit) for i in range(count)])]
    slice x4 -> x1, local copies, waits for them, and re-layouts: 22.1 us -> 0.15 us  [shards(): packed[:, :cut]]
    select_n x12 -> x3, other arithmetic: 16.5 us -> 0.88 us  [the longest x1 0.49 us: shards(): got = lax.ppermute(jnp.where(place == 0, high, low), 'front', swap)]
    pallas_call x0 -> x2, Pallas kernels: none -> 15 us  [the longest x1 8.77 us: grams(): pl.pallas_call(gram_kernel, out_shape=(jax.ShapeDtypeStruct((packed, B),...]
  transfers between devices with their start and end apart: 7 -> 38, of which waited for: 6 -> 18; matrix products, arithmetic and copies ran while one was open for 2% -> 1% of each run, Pallas kernels for 0% -> 2%
where the time goes in v2:
time: 331 us; the launch traced here: 329 us
  waiting for transfers between devices  115 us (35%)
  blocking collectives  101 us (31%)
  Pallas kernels  49.8 us (15%)
  starting transfers between devices  48.8 us (15%)
  other arithmetic  6.67 us (2%)
  between operations  4.62 us (1%)
    ppermute x34, waiting for transfers between devices, flip(): return lax.ppermute(x, 'sub', [(i, i ^ bit) for i in range(count)])  115 us
    all_gather x1, blocking collectives, shards(): every = lax.all_gather(packed_codes, 'sub', axis=0)  101 us
    ppermute x34, starting transfers between devices, flip(): return lax.ppermute(x, 'sub', [(i, i ^ bit) for i in range(count)])  47.5 us
    pallas_call x1, Pallas kernels, chol_solve(): pl.pallas_call(chol_kernel, out_shape=(jax.ShapeDtypeStruct((n, n), F32),...  34.7 us
    pallas_call x1, Pallas kernels, grams(): pl.pallas_call(gram_kernel, out_shape=(jax.ShapeDtypeStruct((packed, B),...  8.77 us
  transfers between devices with their start and end apart: 38, of which 18 were waited for; matrix products, arithmetic and copies ran while one was open for 1% of the time, Pallas kernels for 2%

profile of v2, /device:TPU:0, one launch (start us, length us, event | category | flops | bytes accessed | tf_op | source)
XLA Modules:
  0.0 328.6 jit_solution(16767761163792111421)
XLA Ops:
  0.6 1.4 slice_bitcast_fusion
  2.6 2.6 collective-permute-start.17
  5.1 1.5 collective-permute-start.22
  10.0 8.8 %shard_map.59 = (f32[4608,128]{1,0:T(8,128)}, f32[1024,256]{1,0:T(8,128)S(1)}, f32[1024,256]{1,0:T(8,128)S(1)}, f32[1024,256]{1,0:T(8,128)S(1)}, f32[1024,256]{1,0:T(8,128)S(1)}) custom-call(s32[26]{0:T(128)S(1)} %pad_add_fusion.info_ref, bf16[1,3072,512]{2,1,0:T(8,128)(2,1)} %own_ref.1, bf16[1280,512]{1,0:T(8,128)(2,1)S(1)} %collective-permute-done.other_ref, ...), custom_call_target="tpu_custom_call" | custom-call | flops 4026531840 | bytes 11534336 | tf_op jit(solution)/shard_map/pallas_call | solution.py:210
  19.0 3.4 %collective-permute-start.31 = (f32[2,2,2,64,256]{4,3,2,1,0:T(8,128)S(1)}, f32[2,2,2,64,256]{4,3,2,1,0:T(8,128)S(1)}, u32[]{:S(2)}, u32[]{:S(2)}) collective-permute-start(f32[2,2,2,64,256]{4,3,2,1,0:T(8,128)S(1)} %dynamic-slice_bitcast_fusion.2), channel_id=1, source_target_pairs={{0,4},{2,6},{4,0},{6,2},{8,12},{10,14},{12,8},{14,10},{16,20},{18,... | collective-permute-start | bytes 1572872 | tf_op jit(solution)/shard_map/ppermute | solution.py:279
  22.5 1.9 collective-permute-start.18
  24.9 10.2 %collective-permute-done.31 = f32[2,2,2,64,256]{4,3,2,1,0:T(8,128)S(1)} collective-permute-done((f32[2,2,2,64,256]{4,3,2,1,0:T(8,128)S(1)}, f32[2,2,2,64,256]{4,3,2,1,0:T(8,128)S(1)}, u32[]{:S(2)}, u32[]{:S(2)}) %collective-permute-start.31) | collective-permute-done | bytes 524320 | tf_op jit(solution)/shard_map/ppermute | solution.py:279
  35.1 2.1 collective-permute-start.9
  37.8 8.6 %collective-permute-done.23 = f32[2,2,2,64,256]{4,3,2,1,0:T(8,128)S(1)} collective-permute-done((f32[2,2,2,64,256]{4,3,2,1,0:T(8,128)S(1)}, f32[2,2,2,64,256]{4,3,2,1,0:T(8,128)S(1)}, u32[]{:S(2)}, u32[]{:S(2)}) %collective-permute-start.23) | collective-permute-done | bytes 524320 | tf_op jit(solution)/shard_map/ppermute | solution.py:279
  46.3 2.1 collective-permute-start.28
  49.0 12.1 %collective-permute-done.1 = f32[2,2,2,144,128]{4,3,2,1,0:T(8,128)S(1)} collective-permute-done((f32[2,2,2,144,128]{4,3,2,1,0:T(8,128)S(1)}, f32[2,2,2,144,128]{4,3,2,1,0:T(8,128)S(1)}, u32[]{:S(2)}, u32[]{:S(2)}) %collective-permute-start.1) | collective-permute-done | bytes 589856 | tf_op jit(solution)/shard_map/ppermute | solution.py:279
  61.3 2.1 collective-permute-start.2
  63.4 23.6 %collective-permute-done.2 = f32[2,2,144,128]{3,2,1,0:T(8,128)S(1)} collective-permute-done((f32[2,2,144,128]{3,2,1,0:T(8,128)S(1)}, f32[2,2,144,128]{3,2,1,0:T(8,128)S(1)}, u32[]{:S(2)}, u32[]{:S(2)}) %collective-permute-start.2) | collective-permute-done | bytes 294944 | tf_op jit(solution)/shard_map/ppermute | solution.py:279
  87.0 0.7 collective-permute-start.10
  87.8 7.5 %collective-permute-done.10 = f32[2,2,144,128]{3,2,1,0:T(8,128)S(1)} collective-permute-done((f32[2,2,144,128]{3,2,1,0:T(8,128)S(1)}, f32[2,2,144,128]{3,2,1,0:T(8,128)S(1)}, u32[]{:S(2)}, u32[]{:S(2)}) %collective-permute-start.10) | collective-permute-done | bytes 294944 | tf_op jit(solution)/shard_map/ppermute | solution.py:279
  95.3 1.5 collective-permute-start.3
  97.0 3.5 %collective-permute-done.3 = f32[2,144,128]{2,1,0:T(8,128)S(1)} collective-permute-done((f32[2,144,128]{2,1,0:T(8,128)S(1)}, f32[2,144,128]{2,1,0:T(8,128)S(1)}, u32[]{:S(2)}, u32[]{:S(2)}) %collective-permute-start.3) | collective-permute-done | bytes 147488 | tf_op jit(solution)/shard_map/ppermute | solution.py:279
  100.5 1.6 collective-permute-start.11
  102.1 3.5 %collective-permute-done.11 = f32[2,144,128]{2,1,0:T(8,128)S(1)} collective-permute-done((f32[2,144,128]{2,1,0:T(8,128)S(1)}, f32[2,144,128]{2,1,0:T(8,128)S(1)}, u32[]{:S(2)}, u32[]{:S(2)}) %collective-permute-start.11) | collective-permute-done | bytes 147488 | tf_op jit(solution)/shard_map/ppermute | solution.py:279
  105.6 3.1 collective-permute-start.4
  109.0 1.5 collective-permute-start.33
  110.7 0.7 collective-permute-start.29
  111.5 1.5 collective-permute-start.25
  113.9 1.8 collective-permute-done.12
  115.7 1.2 collective-permute-start.5
  116.9 16.7 %collective-permute-done.5 = f32[144,128]{1,0:T(8,128)S(1)} collective-permute-done((f32[144,128]{1,0:T(8,128)S(1)}, f32[144,128]{1,0:T(8,128)S(1)}, u32[]{:S(2)}, u32[]{:S(2)}) %collective-permute-start.5) | collective-permute-done | bytes 73760 | tf_op jit(solution)/shard_map/ppermute | solution.py:279
  133.5 3.4 %collective-permute-start.13 = (f32[144,128]{1,0:T(8,128)S(1)}, f32[144,128]{1,0:T(8,128)S(1)}, u32[]{:S(2)}, u32[]{:S(2)}) collective-permute-start(f32[144,128]{1,0:T(8,128)S(1)} %bitcast_add_fusion.16), channel_id=1, source_target_pairs={{0,16},{2,18},{4,20},{6,22},{8,24},{10,26},{12,28},{14,30},{16,0},... | collective-permute-start | bytes 221192 | tf_op jit(solution)/shard_map/ppermute | solution.py:279
  137.0 2.7 collective-permute-done.13
  139.6 3.1 collective-permute-start.6
  142.9 2.4 collective-permute-start.34
  145.4 0.7 collective-permute-start.30
  146.2 2.4 collective-permute-start.26
  148.6 1.2 collective-permute-start.21
  149.9 1.3 collective-permute-start.7
  151.2 6.5 %collective-permute-done.34 = f32[2,64,256]{2,1,0:T(8,128)S(1)} collective-permute-done((f32[2,64,256]{2,1,0:T(8,128)S(1)}, f32[2,64,256]{2,1,0:T(8,128)S(1)}, u32[]{:S(2)}, u32[]{:S(2)}) %collective-permute-start.34) | collective-permute-done | bytes 131104 | tf_op jit(solution)/shard_map/ppermute | solution.py:279
  157.7 1.4 collective-permute-start.15
  159.1 1.3 collective-permute-done.30
  160.5 1.4 collective-permute-done.26
  161.9 1.4 collective-permute-done.21
  163.5 1.6 collective-permute-start.8
  165.2 1.4 collective-permute-start.16
  166.8 12.6 %collective-permute-done.8 = f32[2,2,2,144,128]{4,3,2,1,0:T(8,128)S(1)} collective-permute-done((f32[2,2,2,144,128]{4,3,2,1,0:T(8,128)S(1)}, f32[2,2,2,144,128]{4,3,2,1,0:T(8,128)S(1)}, u32[]{:S(2)}, u32[]{:S(2)}) %collective-permute-start.8) | collective-permute-done | bytes 589856 | tf_op jit(solution)/shard_map/ppermute | solution.py:279
  179.5 1.2 collective-permute-done.16
  181.1 34.7 %shard_map.60 = (f32[1024,1024]{1,0:T(8,128)S(1)}, s16[1040,128]{1,0:T(8,128)(2,1)S(1)}) custom-call(f32[4608,128]{1,0:T(8,128)S(1)} %bitcast.284, f32[128,1024]{1,0:T(8,128)S(1)} %pad_maximum_fusion.7.t_ref), custom_call_target="tpu_custom_call" | custom-call | flops 3221225472 | bytes 9437184 | tf_op jit(solution)/shard_map/pallas_call | solution.py:140
  218.0 100.9 %all-gather.1.q_ref.s_ref = s16[16,1040,128]{2,1,0:T(8,128)(2,1)S(1)} all-gather(s16[1,1040,128]{2,1,0:T(8,128)(2,1)S(1)} %add_select_fusion), channel_id=1, replica_groups=mesh['sub'=16,'front'=2] {'sub'}, dimensions={0}, use_global_device_ids=true | all-gather | bytes 4526080 | tf_op jit(solution)/shard_map/all_gather | solution.py:355
  319.0 6.3 %shard_map.61 = f32[2,1024,1024]{2,1,0:T(8,128)} custom-call(s16[16,1040,128]{2,1,0:T(8,128)(2,1)S(1)} %all-gather.1.q_ref.s_ref, s16[16,1040,128]{2,1,0:T(8,128)(2,1)S(1)} %all-gather.1.q_ref.s_ref), custom_call_target="tpu_custom_call" | custom-call | bytes 12648448 | tf_op jit(solution)/shard_map/pallas_call | solution.py:253
  325.2 0.8 select_bitcast_fusion.1
  326.0 2.5 pad_maximum_fusion
  (118 shorter events, 7.7 us)
Async XLA Ops:
  0.6 6.7 %copy-start.1 = (s32[1,24]{1,0:T(1,128)S(1)}, s32[1,24]{1,0:T(1,128)}, u32[]{:S(2)}) copy-start(s32[1,24]{1,0:T(1,128)} %param.6) | copy-start | bytes 292
  2.0 8.0 %collective-permute-start = (bf16[1280,512]{1,0:T(8,128)(2,1)S(1)}, bf16[1280,512]{1,0:T(8,128)(2,1)S(1)}, u32[]{:S(2)}, u32[]{:S(2)}) collective-permute-start(bf16[1280,512]{1,0:T(8,128)(2,1)S(1)} %slice_bitcast_fusion), channel_id=1, source_target_pairs={{0,1},{1,0},{2,3},{3,2},{4,5},{5,4},{6,7},{7,6},{8,9},{9,8},{10,11... | collective-permute-start | bytes 3932168 | tf_op jit(solution)/shard_map/ppermute | solution.py:329
  2.6 4.9 %collective-permute-start.17 = (s32[1]{0:T(128)}, s32[1]{0:T(128)}, u32[]{:S(2)}, u32[]{:S(2)}) collective-permute-start(s32[1]{0:T(128)} %param.7), channel_id=1, source_target_pairs={{0,2},{2,0},{4,6},{6,4},{8,10},{10,8},{12,14},{14,12},{16,18},{18,... | collective-permute-start | bytes 20 | tf_op jit(solution)/shard_map/ppermute | solution.py:279
  5.1 3.6 %collective-permute-start.22 = (s32[1]{0:T(128)}, s32[1]{0:T(128)}, u32[]{:S(2)}, u32[]{:S(2)}) collective-permute-start(s32[1]{0:T(128)} %param.7), channel_id=1, source_target_pairs={{0,4},{2,6},{4,0},{6,2},{8,12},{10,14},{12,8},{14,10},{16,20},{18,... | collective-permute-start | bytes 20 | tf_op jit(solution)/shard_map/ppermute | solution.py:279
  18.8 5.7 %copy-start = (f32[4608,128]{1,0:T(8,128)S(1)}, f32[4608,128]{1,0:T(8,128)}, u32[]{:S(2)}) copy-start(f32[4608,128]{1,0:T(8,128)} %get-tuple-element.9) | copy-start | bytes 7077892
  19.0 16.1 %collective-permute-start.31 = (f32[2,2,2,64,256]{4,3,2,1,0:T(8,128)S(1)}, f32[2,2,2,64,256]{4,3,2,1,0:T(8,128)S(1)}, u32[]{:S(2)}, u32[]{:S(2)}) collective-permute-start(f32[2,2,2,64,256]{4,3,2,1,0:T(8,128)S(1)} %dynamic-slice_bitcast_fusion.2), channel_id=1, source_target_pairs={{0,4},{2,6},{4,0},{6,2},{8,12},{10,14},{12,8},{14,10},{16,20},{18,... | collective-permute-start | bytes 1572872 | tf_op jit(solution)/shard_map/ppermute | solution.py:279
  22.4 15.1 %collective-permute-start.27 = (f32[2,2,2,64,256]{4,3,2,1,0:T(8,128)S(1)}, f32[2,2,2,64,256]{4,3,2,1,0:T(8,128)S(1)}, u32[]{:S(2)}, u32[]{:S(2)}) collective-permute-start(f32[2,2,2,64,256]{4,3,2,1,0:T(8,128)S(1)} %dynamic-slice_bitcast_fusion.3), channel_id=1, source_target_pairs={{0,2},{2,0},{4,6},{6,4},{8,10},{10,8},{12,14},{14,12},{16,18},{18,... | collective-permute-start | bytes 1572872 | tf_op jit(solution)/shard_map/ppermute | solution.py:279
  22.4 23.9 %collective-permute-start.23 = (f32[2,2,2,64,256]{4,3,2,1,0:T(8,128)S(1)}, f32[2,2,2,64,256]{4,3,2,1,0:T(8,128)S(1)}, u32[]{:S(2)}, u32[]{:S(2)}) collective-permute-start(f32[2,2,2,64,256]{4,3,2,1,0:T(8,128)S(1)} %dynamic-slice_bitcast_fusion.4), channel_id=1, source_target_pairs={{0,4},{2,6},{4,0},{6,2},{8,12},{10,14},{12,8},{14,10},{16,20},{18,... | collective-permute-start | bytes 1572872 | tf_op jit(solution)/shard_map/ppermute | solution.py:279
  22.5 26.2 %collective-permute-start.18 = (f32[2,2,2,64,256]{4,3,2,1,0:T(8,128)S(1)}, f32[2,2,2,64,256]{4,3,2,1,0:T(8,128)S(1)}, u32[]{:S(2)}, u32[]{:S(2)}) collective-permute-start(f32[2,2,2,64,256]{4,3,2,1,0:T(8,128)S(1)} %dynamic-slice_bitcast_fusion.5), channel_id=1, source_target_pairs={{0,2},{2,0},{4,6},{6,4},{8,10},{10,8},{12,14},{14,12},{16,18},{18,... | collective-permute-start | bytes 1572872 | tf_op jit(solution)/shard_map/ppermute | solution.py:279
  24.7 36.4 %collective-permute-start.1 = (f32[2,2,2,144,128]{4,3,2,1,0:T(8,128)S(1)}, f32[2,2,2,144,128]{4,3,2,1,0:T(8,128)S(1)}, u32[]{:S(2)}, u32[]{:S(2)}) collective-permute-start(f32[2,2,2,144,128]{4,3,2,1,0:T(8,128)S(1)} %dynamic-slice_bitcast_fusion.1), channel_id=1, source_target_pairs={{0,2},{2,0},{4,6},{6,4},{8,10},{10,8},{12,14},{14,12},{16,18},{18,... | collective-permute-start | bytes 1769480 | tf_op jit(solution)/shard_map/ppermute | solution.py:279
  35.1 26.1 %collective-permute-start.9 = (f32[2,2,2,144,128]{4,3,2,1,0:T(8,128)S(1)}, f32[2,2,2,144,128]{4,3,2,1,0:T(8,128)S(1)}, u32[]{:S(2)}, u32[]{:S(2)}) collective-permute-start(f32[2,2,2,144,128]{4,3,2,1,0:T(8,128)S(1)} %dynamic-slice_bitcast_fusion), channel_id=1, source_target_pairs={{0,4},{2,6},{4,0},{6,2},{8,12},{10,14},{12,8},{14,10},{16,20},{18,... | collective-permute-start | bytes 1769480 | tf_op jit(solution)/shard_map/ppermute | solution.py:279
  37.5 71.3 %collective-permute-start.32 = (f32[2,2,2,64,256]{4,3,2,1,0:T(8,128)S(1)}, f32[2,2,2,64,256]{4,3,2,1,0:T(8,128)S(1)}, u32[]{:S(2)}, u32[]{:S(2)}) collective-permute-start(f32[2,2,2,64,256]{4,3,2,1,0:T(8,128)S(1)} %fusion.1), channel_id=1, source_target_pairs={{0,2},{2,0},{4,6},{6,4},{8,10},{10,8},{12,14},{14,12},{16,18},{18,... | collective-permute-start | bytes 1572872 | tf_op jit(solution)/shard_map/ppermute | solution.py:279
  46.3 62.7 %collective-permute-start.28 = (f32[2,2,2,64,256]{4,3,2,1,0:T(8,128)S(1)}, f32[2,2,2,64,256]{4,3,2,1,0:T(8,128)S(1)}, u32[]{:S(2)}, u32[]{:S(2)}) collective-permute-start(f32[2,2,2,64,256]{4,3,2,1,0:T(8,128)S(1)} %fusion.6), channel_id=1, source_target_pairs={{0,4},{2,6},{4,0},{6,2},{8,12},{10,14},{12,8},{14,10},{16,20},{18,... | collective-permute-start | bytes 1572872 | tf_op jit(solution)/shard_map/ppermute | solution.py:279
  48.7 62.0 %collective-permute-start.24 = (f32[2,2,2,64,256]{4,3,2,1,0:T(8,128)S(1)}, f32[2,2,2,64,256]{4,3,2,1,0:T(8,128)S(1)}, u32[]{:S(2)}, u32[]{:S(2)}) collective-permute-start(f32[2,2,2,64,256]{4,3,2,1,0:T(8,128)S(1)} %fusion.11), channel_id=1, source_target_pairs={{0,2},{2,0},{4,6},{6,4},{8,10},{10,8},{12,14},{14,12},{16,18},{18,... | collective-permute-start | bytes 1572872 | tf_op jit(solution)/shard_map/ppermute | solution.py:279
  61.1 50.4 %collective-permute-start.19 = (f32[2,2,2,64,256]{4,3,2,1,0:T(8,128)S(1)}, f32[2,2,2,64,256]{4,3,2,1,0:T(8,128)S(1)}, u32[]{:S(2)}, u32[]{:S(2)}) collective-permute-start(f32[2,2,2,64,256]{4,3,2,1,0:T(8,128)S(1)} %fusion.16), channel_id=1, source_target_pairs={{0,4},{2,6},{4,0},{6,2},{8,12},{10,14},{12,8},{14,10},{16,20},{18,... | collective-permute-start | bytes 1572872 | tf_op jit(solution)/shard_map/ppermute | solution.py:279
  61.3 25.8 %collective-permute-start.2 = (f32[2,2,144,128]{3,2,1,0:T(8,128)S(1)}, f32[2,2,144,128]{3,2,1,0:T(8,128)S(1)}, u32[]{:S(2)}, u32[]{:S(2)}) collective-permute-start(f32[2,2,144,128]{3,2,1,0:T(8,128)S(1)} %dynamic-slice_bitcast_fusion.7), channel_id=1, source_target_pairs={{0,4},{2,6},{4,0},{6,2},{8,12},{10,14},{12,8},{14,10},{16,20},{18,... | collective-permute-start | bytes 884744 | tf_op jit(solution)/shard_map/ppermute | solution.py:279
  87.0 8.3 %collective-permute-start.10 = (f32[2,2,144,128]{3,2,1,0:T(8,128)S(1)}, f32[2,2,144,128]{3,2,1,0:T(8,128)S(1)}, u32[]{:S(2)}, u32[]{:S(2)}) collective-permute-start(f32[2,2,144,128]{3,2,1,0:T(8,128)S(1)} %dynamic-slice_bitcast_fusion.6), channel_id=1, source_target_pairs={{0,2},{2,0},{4,6},{6,4},{8,10},{10,8},{12,14},{14,12},{16,18},{18,... | collective-permute-start | bytes 884744 | tf_op jit(solution)/shard_map/ppermute | solution.py:279
  95.3 5.1 %collective-permute-start.3 = (f32[2,144,128]{2,1,0:T(8,128)S(1)}, f32[2,144,128]{2,1,0:T(8,128)S(1)}, u32[]{:S(2)}, u32[]{:S(2)}) collective-permute-start(f32[2,144,128]{2,1,0:T(8,128)S(1)} %dynamic-slice_bitcast_fusion.10), channel_id=1, source_target_pairs={{0,8},{2,10},{4,12},{6,14},{8,0},{10,2},{12,4},{14,6},{16,24},{18,... | collective-permute-start | bytes 442376 | tf_op jit(solution)/shard_map/ppermute | solution.py:279
  100.5 5.1 %collective-permute-start.11 = (f32[2,144,128]{2,1,0:T(8,128)S(1)}, f32[2,144,128]{2,1,0:T(8,128)S(1)}, u32[]{:S(2)}, u32[]{:S(2)}) collective-permute-start(f32[2,144,128]{2,1,0:T(8,128)S(1)} %dynamic-slice_bitcast_fusion.9), channel_id=1, source_target_pairs={{0,8},{2,10},{4,12},{6,14},{8,0},{10,2},{12,4},{14,6},{16,24},{18,... | collective-permute-start | bytes 442376 | tf_op jit(solution)/shard_map/ppermute | solution.py:279
  105.6 7.5 %collective-permute-start.4 = (f32[144,128]{1,0:T(8,128)S(1)}, f32[144,128]{1,0:T(8,128)S(1)}, u32[]{:S(2)}, u32[]{:S(2)}) collective-permute-start(f32[144,128]{1,0:T(8,128)S(1)} %dynamic-slice_bitcast_fusion.16), channel_id=1, source_target_pairs={{0,16},{2,18},{4,20},{6,22},{8,24},{10,26},{12,28},{14,30},{16,0},... | collective-permute-start | bytes 221192 | tf_op jit(solution)/shard_map/ppermute | solution.py:279
  108.8 6.9 %collective-permute-start.12 = (f32[144,128]{1,0:T(8,128)S(1)}, f32[144,128]{1,0:T(8,128)S(1)}, u32[]{:S(2)}, u32[]{:S(2)}) collective-permute-start(f32[144,128]{1,0:T(8,128)S(1)} %dynamic-slice_bitcast_fusion.15), channel_id=1, source_target_pairs={{0,16},{2,18},{4,20},{6,22},{8,24},{10,26},{12,28},{14,30},{16,0},... | collective-permute-start | bytes 221192 | tf_op jit(solution)/shard_map/ppermute | solution.py:279
  109.0 33.7 %collective-permute-start.33 = (f32[2,2,64,256]{3,2,0,1:T(8,128)S(1)}, f32[2,2,64,256]{3,2,0,1:T(8,128)S(1)}, u32[]{:S(2)}, u32[]{:S(2)}) collective-permute-start(f32[2,2,64,256]{3,2,0,1:T(8,128)S(1)} %bitcast.300), channel_id=1, source_target_pairs={{0,8},{2,10},{4,12},{6,14},{8,0},{10,2},{12,4},{14,6},{16,24},{18,... | collective-permute-start | bytes 786440 | tf_op jit(solution)/shard_map/ppermute | solution.py:279
  110.7 32.3 %collective-permute-start.29 = (f32[2,2,64,256]{3,2,0,1:T(8,128)S(1)}, f32[2,2,64,256]{3,2,0,1:T(8,128)S(1)}, u32[]{:S(2)}, u32[]{:S(2)}) collective-permute-start(f32[2,2,64,256]{3,2,0,1:T(8,128)S(1)} %bitcast.301), channel_id=1, source_target_pairs={{0,8},{2,10},{4,12},{6,14},{8,0},{10,2},{12,4},{14,6},{16,24},{18,... | collective-permute-start | bytes 786440 | tf_op jit(solution)/shard_map/ppermute | solution.py:279
  111.5 33.9 %collective-permute-start.25 = (f32[2,2,64,256]{3,2,0,1:T(8,128)S(1)}, f32[2,2,64,256]{3,2,0,1:T(8,128)S(1)}, u32[]{:S(2)}, u32[]{:S(2)}) collective-permute-start(f32[2,2,64,256]{3,2,0,1:T(8,128)S(1)} %bitcast.302), channel_id=1, source_target_pairs={{0,8},{2,10},{4,12},{6,14},{8,0},{10,2},{12,4},{14,6},{16,24},{18,... | collective-permute-start | bytes 786440 | tf_op jit(solution)/shard_map/ppermute | solution.py:279
  113.2 33.0 %collective-permute-start.20 = (f32[2,2,64,256]{3,2,0,1:T(8,128)S(1)}, f32[2,2,64,256]{3,2,0,1:T(8,128)S(1)}, u32[]{:S(2)}, u32[]{:S(2)}) collective-permute-start(f32[2,2,64,256]{3,2,0,1:T(8,128)S(1)} %bitcast.303), channel_id=1, source_target_pairs={{0,8},{2,10},{4,12},{6,14},{8,0},{10,2},{12,4},{14,6},{16,24},{18,... | collective-permute-start | bytes 786440 | tf_op jit(solution)/shard_map/ppermute | solution.py:279
  115.7 17.9 %collective-permute-start.5 = (f32[144,128]{1,0:T(8,128)S(1)}, f32[144,128]{1,0:T(8,128)S(1)}, u32[]{:S(2)}, u32[]{:S(2)}) collective-permute-start(f32[144,128]{1,0:T(8,128)S(1)} %bitcast_add_fusion.17), channel_id=1, source_target_pairs={{0,16},{2,18},{4,20},{6,22},{8,24},{10,26},{12,28},{14,30},{16,0},... | collective-permute-start | bytes 221192 | tf_op jit(solution)/shard_map/ppermute | solution.py:279
  133.5 6.1 %collective-permute-start.13 = (f32[144,128]{1,0:T(8,128)S(1)}, f32[144,128]{1,0:T(8,128)S(1)}, u32[]{:S(2)}, u32[]{:S(2)}) collective-permute-start(f32[144,128]{1,0:T(8,128)S(1)} %bitcast_add_fusion.16), channel_id=1, source_target_pairs={{0,16},{2,18},{4,20},{6,22},{8,24},{10,26},{12,28},{14,30},{16,0},... | collective-permute-start | bytes 221192 | tf_op jit(solution)/shard_map/ppermute | solution.py:279
  139.6 9.0 %collective-permute-start.6 = (f32[2,144,128]{2,1,0:T(8,128)S(1)}, f32[2,144,128]{2,1,0:T(8,128)S(1)}, u32[]{:S(2)}, u32[]{:S(2)}) collective-permute-start(f32[2,144,128]{2,1,0:T(8,128)S(1)} %pad_maximum_fusion.10), channel_id=1, source_target_pairs={{0,8},{2,10},{4,12},{6,14},{8,0},{10,2},{12,4},{14,6},{16,24},{18,... | collective-permute-start | bytes 442376 | tf_op jit(solution)/shard_map/ppermute | solution.py:279
  142.8 7.1 %collective-permute-start.14 = (f32[2,144,128]{2,1,0:T(8,128)S(1)}, f32[2,144,128]{2,1,0:T(8,128)S(1)}, u32[]{:S(2)}, u32[]{:S(2)}) collective-permute-start(f32[2,144,128]{2,1,0:T(8,128)S(1)} %pad_maximum_fusion.11), channel_id=1, source_target_pairs={{0,8},{2,10},{4,12},{6,14},{8,0},{10,2},{12,4},{14,6},{16,24},{18,... | collective-permute-start | bytes 442376 | tf_op jit(solution)/shard_map/ppermute | solution.py:279
  142.9 14.7 %collective-permute-start.34 = (f32[2,64,256]{2,1,0:T(8,128)S(1)}, f32[2,64,256]{2,1,0:T(8,128)S(1)}, u32[]{:S(2)}, u32[]{:S(2)}) collective-permute-start(f32[2,64,256]{2,1,0:T(8,128)S(1)} %dynamic-slice_bitcast_fusion.11), channel_id=1, source_target_pairs={{0,16},{2,18},{4,20},{6,22},{8,24},{10,26},{12,28},{14,30},{16,0},... | collective-permute-start | bytes 393224 | tf_op jit(solution)/shard_map/ppermute | solution.py:279
  145.4 15.1 %collective-permute-start.30 = (f32[2,64,256]{2,1,0:T(8,128)S(1)}, f32[2,64,256]{2,1,0:T(8,128)S(1)}, u32[]{:S(2)}, u32[]{:S(2)}) collective-permute-start(f32[2,64,256]{2,1,0:T(8,128)S(1)} %dynamic-slice_bitcast_fusion.12), channel_id=1, source_target_pairs={{0,16},{2,18},{4,20},{6,22},{8,24},{10,26},{12,28},{14,30},{16,0},... | collective-permute-start | bytes 393224 | tf_op jit(solution)/shard_map/ppermute | solution.py:279
  146.2 15.7 %collective-permute-start.26 = (f32[2,64,256]{2,1,0:T(8,128)S(1)}, f32[2,64,256]{2,1,0:T(8,128)S(1)}, u32[]{:S(2)}, u32[]{:S(2)}) collective-permute-start(f32[2,64,256]{2,1,0:T(8,128)S(1)} %dynamic-slice_bitcast_fusion.13), channel_id=1, source_target_pairs={{0,16},{2,18},{4,20},{6,22},{8,24},{10,26},{12,28},{14,30},{16,0},... | collective-permute-start | bytes 393224 | tf_op jit(solution)/shard_map/ppermute | solution.py:279
  148.6 14.6 %collective-permute-start.21 = (f32[2,64,256]{2,1,0:T(8,128)S(1)}, f32[2,64,256]{2,1,0:T(8,128)S(1)}, u32[]{:S(2)}, u32[]{:S(2)}) collective-permute-start(f32[2,64,256]{2,1,0:T(8,128)S(1)} %dynamic-slice_bitcast_fusion.14), channel_id=1, source_target_pairs={{0,16},{2,18},{4,20},{6,22},{8,24},{10,26},{12,28},{14,30},{16,0},... | collective-permute-start | bytes 393224 | tf_op jit(solution)/shard_map/ppermute | solution.py:279
  149.9 13.6 %collective-permute-start.7 = (f32[2,2,144,128]{3,2,1,0:T(8,128)S(1)}, f32[2,2,144,128]{3,2,1,0:T(8,128)S(1)}, u32[]{:S(2)}, u32[]{:S(2)}) collective-permute-start(f32[2,2,144,128]{3,2,1,0:T(8,128)S(1)} %pad_maximum_fusion.8), channel_id=1, source_target_pairs={{0,4},{2,6},{4,0},{6,2},{8,12},{10,14},{12,8},{14,10},{16,20},{18,... | collective-permute-start | bytes 884744 | tf_op jit(solution)/shard_map/ppermute | solution.py:279
  157.7 7.4 %collective-permute-start.15 = (f32[2,2,144,128]{3,2,1,0:T(8,128)S(1)}, f32[2,2,144,128]{3,2,1,0:T(8,128)S(1)}, u32[]{:S(2)}, u32[]{:S(2)}) collective-permute-start(f32[2,2,144,128]{3,2,1,0:T(8,128)S(1)} %pad_maximum_fusion.9), channel_id=1, source_target_pairs={{0,2},{2,0},{4,6},{6,4},{8,10},{10,8},{12,14},{14,12},{16,18},{18,... | collective-permute-start | bytes 884744 | tf_op jit(solution)/shard_map/ppermute | solution.py:279
  163.4 3.3 %collective-permute-start.35 = (f32[64,1024]{1,0:T(8,128)S(1)}, f32[64,1024]{1,0:T(8,128)S(1)}, u32[]{:S(2)}, u32[]{:S(2)}) collective-permute-start(f32[64,1024]{1,0:T(8,128)S(1)} %dynamic-slice_bitcast_fusion.8), channel_id=1, source_target_pairs={{0,1},{1,0},{2,3},{3,2},{4,5},{5,4},{6,7},{7,6},{8,9},{9,8},{10,11... | collective-permute-start | bytes 786440 | tf_op jit(solution)/shard_map/ppermute | solution.py:344
  163.5 15.8 %collective-permute-start.8 = (f32[2,2,2,144,128]{4,3,2,1,0:T(8,128)S(1)}, f32[2,2,2,144,128]{4,3,2,1,0:T(8,128)S(1)}, u32[]{:S(2)}, u32[]{:S(2)}) collective-permute-start(f32[2,2,2,144,128]{4,3,2,1,0:T(8,128)S(1)} %pad_maximum_fusion.4), channel_id=1, source_target_pairs={{0,2},{2,0},{4,6},{6,4},{8,10},{10,8},{12,14},{14,12},{16,18},{18,... | collective-permute-start | bytes 1769480 | tf_op jit(solution)/shard_map/ppermute | solution.py:279
  165.2 15.5 %collective-permute-start.16 = (f32[2,2,2,144,128]{4,3,2,1,0:T(8,128)S(1)}, f32[2,2,2,144,128]{4,3,2,1,0:T(8,128)S(1)}, u32[]{:S(2)}, u32[]{:S(2)}) collective-permute-start(f32[2,2,2,144,128]{4,3,2,1,0:T(8,128)S(1)} %pad_maximum_fusion.5), channel_id=1, source_target_pairs={{0,4},{2,6},{4,0},{6,2},{8,12},{10,14},{12,8},{14,10},{16,20},{18,... | collective-permute-start | bytes 1769480 | tf_op jit(solution)/shard_map/ppermute | solution.py:279
  215.9 1.6 collective-permute-start.37
  216.4 108.8 %collective-permute-start.36 = (f32[1024,512]{1,0:T(8,128)S(1)}, f32[1024,512]{1,0:T(8,128)S(1)}, u32[]{:S(2)}, u32[]{:S(2)}) collective-permute-start(f32[1024,512]{1,0:T(8,128)S(1)} %slice_select_fusion), channel_id=1, source_target_pairs={{0,1},{1,0},{2,3},{3,2},{4,5},{5,4},{6,7},{7,6},{8,9},{9,8},{10,11... | collective-permute-start | bytes 6291464 | tf_op jit(solution)/shard_map/ppermute | solution.py:360

commit v3 on v2

v3 whole, which is shorter than its diff:
```python
import jax, jax.numpy as jnp
from jax import lax
from jax.experimental import pallas as pl
from jax.experimental.pallas import tpu as pltpu
from jax.sharding import PartitionSpec as P
B=128
F32=jnp.float32
BF=jnp.bfloat16
LIVE = 1280
NPAR = 2
PIECES = 4
LEVELS = 32766.0
SWAP = [(0, 1), (1, 0)]

def split(x):
    hi = x.astype(BF)
    return hi, (x - hi.astype(F32)).astype(BF)

def factor_block(d_ref, w_ref, fillers):
    rows8 = (8, B)
    for g in range(B // 8):
        xs, xi = [], []
        for i in range(8):
            row = d_ref[8*g+i:8*g+i+1, :]
            xs.append(jnp.broadcast_to(row[:, :B], rows8))
            xi.append(jnp.broadcast_to(row[:, B:], rows8))
        s = {}
        for i in range(8):
            for j in range(i, 8):
                s[i, j] = jnp.broadcast_to(xs[i][:, 8*g+j:8*g+j+1], rows8)
        for i in range(8):
            rs = lax.rsqrt(s[i, i])
            inv = rs * rs
            w_ref[8*g+i:8*g+i+1, :B] = (xs[i] * rs)[:1]
            w_ref[8*g+i:8*g+i+1, B:] = (xi[i] * rs)[:1]
            for r in range(8):
                if r == i: continue
                m = (s[r, i] if r < i else s[i, r]) * inv
                for j in range(max(r, i+1), 8):
                    s[r, j] = s[r, j] - m * s[i, j]
                xs[r] = xs[r] - m * xs[i]
                xi[r] = xi[r] - m * xi[i]
            s[i, i] = inv
        ys = [xs[i] * s[i, i] for i in range(8)]
        yi = [xi[i] * s[i, i] for i in range(8)]
        for r in range(g+1, B // 8):
            blk = d_ref[8*r:8*r+8, :B]
            bi = d_ref[8*r:8*r+8, B:]
            cols = [jnp.broadcast_to(blk[:, 8*g+i:8*g+i+1], rows8) for i in range(8)]
            for i in range(8):
                blk = blk - cols[i] * ys[i]
                bi = bi - cols[i] * yi[i]
            d_ref[8*r:8*r+8, :B] = blk
            d_ref[8*r:8*r+8, B:] = bi
        if fillers:
            fillers.pop(0)()
    while fillers:
        fillers.pop(0)()


def gram_rows(i, j):
    t = j // 2
    return j % 2, (t * t + t + i) * B


def chol_kernel(first, last, *refs):
    begin = first == 0
    if begin:
        g_ref, t_ref, *refs = refs
    else:
        in_ref, *refs = refs
    r_ref, q_ref, *refs = refs
    if begin:
        out_ref, *refs = refs
    s_ref, z_ref, d_ref, w_ref, rhs_ref = refs
    nt = z_ref.shape[1]
    n = r_ref.shape[1]
    nb = n // B
    base = first * B
    ri = lax.broadcasted_iota(jnp.int32, (B, B), 0)
    ci = lax.broadcasted_iota(jnp.int32, (B, B), 1)

    def gram_block(i, j):
        core, at = gram_rows(i, j)
        share = g_ref.shape[2]
        parts, end = [], at + B
        while at < end:
            chip, off = at // share, at % share
            size = min(share - off, end - at)
            parts.append(g_ref[chip, core, off:off+size, :])
            at += size
        return parts[0] if len(parts) == 1 else jnp.concatenate(parts, axis=0)

    def left(i, lo, hi):
        if not begin:
            return in_ref[(i-first)*B:(i-first+1)*B, lo-base:hi-base]
        if lo >= n:
            return jnp.transpose(t_ref[:, i*B:(i+1)*B])
        parts = [gram_block(i, j) for j in range(lo // B, min(hi, n) // B)]
        if hi > n:
            parts.append(jnp.transpose(t_ref[:, i*B:(i+1)*B]))
        return parts[0] if len(parts) == 1 else jnp.concatenate(parts, axis=1)

    def current(k, lo, hi):
        return left(k, lo, hi) if k == first else s_ref[k*B-base:(k+1)*B-base, lo-base:hi-base]

    def update(k, i):
        def run():
            lo = i * B
            lhs = split(jnp.transpose(r_ref[k*B-base:(k+1)*B-base, lo:lo+B]))
            lhs = jnp.concatenate([lhs[0], lhs[0], lhs[1]], axis=1)
            upd = jnp.dot(lhs, rhs_ref[k % 2, :, lo-base:], preferred_element_type=F32)
            new = current(i, lo, n + nt) - upd if k > first else left(i, lo, n + nt) - upd
            if i >= last and k == last - 1:
                out_ref[(i-last)*B:(i-last+1)*B, lo-last*B:] = new
            else:
                s_ref[lo-base:lo-base+B, lo-base:] = new
        return run

    fillers = []
    for k in range(first, last):
        lo = k * B
        at = lo - base
        d_ref[:, :B] = current(k, lo, lo + B)
        d_ref[:, B:] = jnp.where(ri == ci, 1.0, 0.0).astype(F32)
        factor_block(d_ref, w_ref, fillers)
        fillers = []
        if k:
            r_ref[at:at+B, :lo] = jnp.zeros((B, lo), F32)
        r_ref[at:at+B, lo:lo+B] = jnp.where(ci >= ri, w_ref[:, :B], 0.0)
        wh, wl = split(w_ref[:, B:])
        w3 = jnp.concatenate([wh, wh, wl], axis=1)
        rh, rl = split(current(k, lo + B, n + nt))
        p = jnp.dot(w3, jnp.concatenate([rh, rl, rh], axis=0), preferred_element_type=F32)
        if k < nb - 1:
            r_ref[at:at+B, lo+B:] = p[:, :n-lo-B]
        z_ref[at:at+B, :] = p[:, n-lo-B:]
        ph, pll = split(p)
        rhs_ref[k % 2, 0:B, lo+B-base:] = ph
        rhs_ref[k % 2, B:2*B, lo+B-base:] = pll
        rhs_ref[k % 2, 2*B:, lo+B-base:] = ph
        if k < nb - 1:
            update(k, k+1)()
            fillers = [update(k, i) for i in range(k+2, nb)]
    for fill in fillers:
        fill()
    count = last - first
    codes, scales = [], []
    for k in range(count):
        z = z_ref[k*B:(k+1)*B, :]
        top = jnp.maximum(jnp.max(jnp.abs(z), axis=0, keepdims=True), 1e-30)
        e = jnp.ceil(jnp.log2(top))
        mant = jnp.minimum(jnp.ceil(top * jnp.exp2(-e) * 16384.0) + 1.0, 32767.0)
        step = mant * jnp.exp2(e) * (1.0 / (16384.0 * LEVELS))
        codes.append(jnp.clip(jnp.round(z * (1.0 / step)), -LEVELS, LEVELS).astype(jnp.int32))
        scales.append(join(e.astype(jnp.int32), mant.astype(jnp.int32)))
    for k in range(count // 2):
        q_ref[k*B:(k+1)*B, :] = join(codes[k], codes[k + count // 2])
    scales += [jnp.zeros_like(scales[0])] * (8 - count)
    q_ref[count//2*B:, :] = jnp.concatenate(scales, axis=0)


def join(high, low):
    return jnp.bitwise_or(jnp.left_shift(high, 16), jnp.bitwise_and(low, 65535))


def high_low(word):
    return jnp.right_shift(word, 16), jnp.right_shift(jnp.left_shift(word, 16), 16)


def chol_rows(first, last, n, nt, *args):
    vmem = pl.BlockSpec(memory_space=pltpu.VMEM)
    rows = (last - first) * B
    wide = n + nt - first * B
    outs = [jax.ShapeDtypeStruct((rows, n), F32), jax.ShapeDtypeStruct((rows // 2 + 8, nt), jnp.int32)]
    if first == 0:
        outs.append(jax.ShapeDtypeStruct((n - last * B, n + nt - last * B), F32))
    return pl.pallas_call(
        lambda *refs: chol_kernel(first, last, *refs),
        out_shape=tuple(outs),
        in_specs=[vmem] * len(args),
        out_specs=(vmem,) * len(outs),
        scratch_shapes=[
            pltpu.VMEM((n - first * B, wide), F32),
            pltpu.VMEM((rows, nt), F32),
            pltpu.VMEM((B, 2*B), F32),
            pltpu.VMEM((B, 2*B), F32),
            pltpu.VMEM((2, 3*B, wide), BF),
        ],
        compiler_params=pltpu.CompilerParams(vmem_limit_bytes=40*1024*1024),
        cost_estimate=pl.CostEstimate(flops=30*n*n*n // 2, bytes_accessed=4*rows*n, transcendentals=0),
    )(*args)


DIMS = (((0,), (0,)), ((), ()))


def pivot_kernel(info_ref, own_ref, other_ref, g_ref, a_ref):
    live, tile = other_ref.shape
    n = a_ref.shape[1]
    place = info_ref[info_ref.shape[0] - 1]
    rows = lax.broadcasted_iota(jnp.int32, (live, B), 0)
    zero = jnp.zeros((live, B), BF)
    per = tile // B
    for half, ref in ((place, own_ref.at[0]), (1 - place, other_ref)):
        for j in range(per):
            end = info_ref[half * per + j]
            at = pl.multiple_of(half * tile + j * B, B)
            a_ref[:, pl.ds(at, B)] = jnp.where(rows < end, ref[:, j*B:(j+1)*B], zero)
    for t in range(n // B // 2):
        at = pl.multiple_of((2 * t + place) * B, B)
        out = lax.dot_general(a_ref[:, :(2*t+2)*B], a_ref[:, pl.ds(at, B)], DIMS, preferred_element_type=F32)
        g_ref[(t*t+t)*B:(t*t+3*t+2)*B, :] = out


def trail_kernel(info_ref, a_ref, trail_ref, *t_refs):
    live, n = a_ref.shape
    place = info_ref[info_ref.shape[0] - 1]
    rows = lax.broadcasted_iota(jnp.int32, (live, B), 0)
    zero = jnp.zeros((live, B), BF)
    per = trail_ref.shape[2] // B
    piece = t_refs[0].shape[1]
    for j in range(0, per, 2):
        cols = []
        for h in (j, j + 1):
            end = info_ref[n // B + place * per + h]
            cols.append(jnp.where(rows < end, trail_ref[0, :, h*B:(h+1)*B], zero))
        out = lax.dot_general(jnp.concatenate(cols, axis=1), a_ref[...], DIMS, preferred_element_type=F32)
        for q, t_ref in enumerate(t_refs):
            t_ref[j*B:(j+2)*B, :] = out[:, q*piece:(q+1)*piece]


def one_step(kernel, info, args, blocks, outs, cost):
    return pl.pallas_call(
        kernel,
        out_shape=tuple(outs),
        grid_spec=pltpu.PrefetchScalarGridSpec(
            num_scalar_prefetch=1,
            grid=(1,),
            in_specs=[pl.BlockSpec(block, lambda i, info, zeros=(0,) * len(block): zeros) for block in blocks],
            out_specs=tuple(pl.BlockSpec(out.shape, lambda i, info: (0, 0)) for out in outs),
        ),
        compiler_params=pltpu.CompilerParams(vmem_limit_bytes=40*1024*1024),
        cost_estimate=pl.CostEstimate(flops=cost, bytes_accessed=16*1024*1024, transcendentals=0),
    )(info, *args)


def pivot_gram(info, piv, other):
    live, tile = other.shape
    n = 2 * tile
    half = n // B // 2
    outs = [jax.ShapeDtypeStruct(((half * half + half) * B, B), F32), jax.ShapeDtypeStruct((live, n), BF)]
    return one_step(pivot_kernel, info, (piv, other), [(1, live, tile), (live, tile)], outs, live*n*n)


def trail_gram(info, masked, trail, pieces):
    live, n = masked.shape
    wide = trail.shape[2]
    outs = [jax.ShapeDtypeStruct((wide, n // pieces), F32)] * pieces
    return one_step(trail_kernel, info, (masked, trail), [(live, n), (1, live, wide)], outs, 2*live*n*wide)


def step_of(word):
    e, mant = high_low(word)
    return mant.astype(F32) * jnp.exp2(e.astype(F32)) * (1.0 / (16384.0 * LEVELS))


def unpack_kernel(q_ref, s_ref, *rest):
    o_ref = rest[-1]
    chips, rows, lanes = q_ref.shape
    half = lanes // 2
    lane = lax.broadcasted_iota(jnp.int32, (rows, lanes), 1)
    which = lax.broadcasted_iota(jnp.int32, (8, lanes), 0)
    blocks = pl.num_programs(0)

    def values(c):
        steps = step_of(s_ref[c])
        picked = [jnp.sum(jnp.where(which == pl.program_id(0) + h * blocks, steps, 0.0), axis=0, keepdims=True) for h in (0, 1)]
        return [v.astype(F32) * step for v, step in zip(high_low(q_ref[c]), picked)]

    for c in range(0, chips, 2):
        for h, (a, b) in enumerate(zip(values(c), values(c + 1))):
            at = c * half
            o_ref[0, 0, h, :, at:at+lanes] = jnp.where(lane < half, a, pltpu.roll(b, half, 1))
            o_ref[1, 0, h, :, at:at+lanes] = jnp.where(lane < half, pltpu.roll(a, half, 1), b)


def unpack(q, part, parts, before):
    chips, rows, lanes = q.shape
    rows -= 8
    wide = chips * lanes // 2
    blocks = rows // B
    args, specs = [q, q], [
        pl.BlockSpec((chips, B, lanes), lambda k: (0, k, 0)),
        pl.BlockSpec((chips, 8, lanes), lambda k: (0, rows // 8, 0)),
    ]
    if before is not None:
        args.append(before)
        specs.append(pl.BlockSpec(memory_space=pl.ANY))
    return pl.pallas_call(
        unpack_kernel,
        out_shape=jax.ShapeDtypeStruct((NPAR, parts, 2, rows, wide), F32),
        grid=(blocks,),
        in_specs=specs,
        out_specs=pl.BlockSpec((NPAR, 1, 2, B, wide), lambda k: (0, part, 0, k, 0)),
        input_output_aliases={} if before is None else {2: 0},
        compiler_params=pltpu.CompilerParams(vmem_limit_bytes=40*1024*1024),
        cost_estimate=pl.CostEstimate(flops=0, bytes_accessed=4*q.size+16*rows*wide, transcendentals=0),
    )(*args)


def unpack_plain(q):
    chips, rows, lanes = q.shape
    rows -= 8
    blocks = rows // B
    step = step_of(q[:, rows:rows+2*blocks]).reshape(chips, 2, blocks, 1, lanes)
    z = jnp.stack(high_low(q[:, :rows]), axis=1).astype(F32).reshape(chips, 2, blocks, B, lanes) * step
    z = z.reshape(chips, 2 * rows, NPAR, lanes // NPAR)
    return jnp.transpose(z, (2, 1, 0, 3)).reshape(NPAR, 2 * rows, chips * lanes // NPAR)


def take(x, axis, index):
    return lax.dynamic_index_in_dim(x, index, axis, keepdims=False)


def flip(x, bit, count):
    return lax.ppermute(x, "sub", [(i, i ^ bit) for i in range(count)])


def halve(x, axis, bit, me, count):
    own = jnp.where(me & bit, 1, 0)
    return take(x, axis, own) + flip(take(x, axis, 1 - own), bit, count)


def bit_orders(count):
    bits = [1 << i for i in range(count.bit_length() - 1)]
    plane = len(bits) // 2
    other = bits[:plane][::-1] + bits[plane:]
    return bits, other


def sum_shares(x, order, me, count, parent, partner):
    left = [1 << i for i in range(count.bit_length() - 1)][::-1]
    x = x.reshape((2,) * len(left) + (x.shape[0] // count, x.shape[1]))
    bit = order[0]
    axis = left.index(bit)
    own = jnp.where(me & bit, 1, 0)
    got = flip(take(x, axis, 1 - own), bit, count)
    kept = take(x, axis, own)
    left.remove(bit)
    x = jnp.stack([jnp.where(parent == p, kept, 0.0) + jnp.where(partner == p, got, 0.0) for p in range(NPAR)])
    for bit in order[1:]:
        x = halve(x, 1 + left.index(bit), bit, me, count)
        left.remove(bit)
    return x


def trade(mine, place):
    keep = take(mine, 0, place)
    got = lax.ppermute(take(mine, 0, 1 - place), "front", SWAP)
    return jnp.stack([jnp.where(place == 0, keep, got), jnp.where(place == 0, got, keep)])


def shards(count, piv_cols, trail_cols, row_end, parent_of):
    place = lax.axis_index("front")
    me = lax.axis_index("sub")
    tile_pivot = piv_cols.shape[2]
    n = NPAR * tile_pivot
    orders = bit_orders(count)
    other_piv = lax.ppermute(piv_cols[0, :LIVE], "front", SWAP)
    parent = parent_of[0]
    partners = [flip(parent_of, order[0], count)[0] for order in orders]
    info = jnp.concatenate([row_end[0], place[None].astype(jnp.int32)])
    packed, masked = pivot_gram(info, piv_cols, other_piv)
    trails = trail_gram(info, masked, trail_cols, PIECES)

    rows = packed.shape[0] // count
    packed = packed.reshape(count, rows, B)
    cut = rows // 16 * 8
    halves = (packed[:, :cut].reshape(-1, B), packed[:, cut:].reshape(-1, B))
    parts = [sum_shares(part, order, me, count, parent, partner) for part, order, partner in zip(halves, orders, partners)]
    gram = lax.all_gather(trade(jnp.concatenate(parts, axis=1), place), "sub", axis=0)

    shares = [sum_shares(t, orders[q % 2], me, count, parent, partners[q % 2]) for q, t in enumerate(trails)]
    share = jnp.concatenate(shares, axis=2)
    width = share.shape[1]
    trail = trade(share, place).reshape(NPAR * width, n)

    def gather(codes):
        theirs = lax.ppermute(codes, "front", SWAP)
        words = jnp.where(
            place == 0,
            jnp.concatenate([codes[:, :width], theirs[:, :width]], axis=1),
            jnp.concatenate([theirs[:, width:], codes[:, width:]], axis=1),
        )
        return lax.all_gather(words, "sub", axis=0)

    def own_columns(factor):
        return trade(jnp.stack([factor[:, :tile_pivot], factor[:, tile_pivot:]]), place)

    nb = n // B
    upper, codes, rest = chol_rows(0, nb // 2, n, NPAR * width, gram, trail)
    first = gather(codes)
    lower, codes = chol_rows(nb // 2, nb, n, NPAR * width, rest)
    second = gather(codes)
    if 2 * width == B:
        r_trail = unpack(second, 1, 2, unpack(first, 0, 2, None)).reshape(NPAR, n, -1)
    else:
        r_trail = jnp.concatenate([unpack_plain(first), unpack_plain(second)], axis=1)
    r_pivot = jnp.concatenate([own_columns(upper), own_columns(lower)], axis=1)
    return (r_pivot, r_trail)


def solution(mesh):
    count = mesh.shape["sub"]
    return jax.shard_map(
        lambda *args: shards(count, *args),
        mesh=mesh,
        in_specs=(P("sub", None, "front"), P("sub", None, "front"), P("sub", None), P("sub")),
        out_specs=(P(None, None, "front"), P(None, None, "front")),
        check_vma=False,
    )
```

time: 331 us -> 332 us (level)
  blocking collectives: 101 us -> 0 us
  waiting for transfers between devices: 115 us -> 185 us
  local copies, waits for them, and re-layouts: 2.72 us -> 17.7 us
  between operations: 4.62 us -> 17.7 us
  Pallas kernels: 49.8 us -> 58.7 us
  starting transfers between devices: 48.8 us -> 41.3 us
  other arithmetic: 6.67 us -> 11.1 us
    all_gather x0 -> x3, waiting for transfers between devices: none -> 112 us  [the longest x2 89.1 us: gather(): return lax.all_gather(words, 'sub', axis=0)]
    all_gather x1 -> x0, blocking collectives: 101 us -> none  [shards(): every = lax.all_gather(packed_codes, 'sub', axis=0)]
    ppermute x34 -> x26, waiting for transfers between devices: 115 us -> 67 us  [flip(): return lax.ppermute(x, 'sub', [(i, i ^ bit) for i in range(count)])]
    unnamed x4 -> x20, local copies, waits for them, and re-layouts: 0.01 us -> 11.6 us
    pallas_call x3 -> x6, Pallas kernels: 49.8 us -> 58.7 us  [the longest x2 46 us: chol_rows(): pl.pallas_call(lambda *refs: chol_kernel(first, last, *refs), out_shape=t...]
    ppermute x34 -> x26, starting transfers between devices: 47.5 us -> 39.7 us  [flip(): return lax.ppermute(x, 'sub', [(i, i ^ bit) for i in range(count)])]
    ppermute x4 -> x7, waiting for transfers between devices: 0.28 us -> 6.01 us  [the longest x4 3.65 us: trade(): got = lax.ppermute(take(mine, 0, 1 - place), 'front', SWAP)]
  transfers between devices with their start and end apart: 38 -> 36, of which waited for: 18 -> 22; matrix products, arithmetic and copies ran while one was open for 1% -> 4% of each run, Pallas kernels for 2% -> 7%
where the time goes in v3:
time: 332 us; the launch traced here: 331 us
  waiting for transfers between devices  185 us (56%)
  Pallas kernels  58.7 us (18%)
  starting transfers between devices  41.3 us (12%)
  local copies, waits for them, and re-layouts  17.7 us (5%)
  between operations  17.7 us (5%)
  other arithmetic  11.1 us (3%)
    all_gather x2, waiting for transfers between devices, gather(): return lax.all_gather(words, 'sub', axis=0)  89.1 us
    ppermute x26, waiting for transfers between devices, flip(): return lax.ppermute(x, 'sub', [(i, i ^ bit) for i in range(count)])  67 us
    pallas_call x2, Pallas kernels, chol_rows(): pl.pallas_call(lambda *refs: chol_kernel(first, last, *refs), out_shape=t...  46 us
    ppermute x26, starting transfers between devices, flip(): return lax.ppermute(x, 'sub', [(i, i ^ bit) for i in range(count)])  39.7 us
    all_gather x1, waiting for transfers between devices, shards(): lax.all_gather(trade(jnp.concatenate(parts, axis=1), place), 'sub', axis=0)  22.7 us
    unnamed x20, local copies, waits for them, and re-layouts  11.6 us
    pallas_call x2, Pallas kernels, one_step(): pl.pallas_call(kernel, out_shape=tuple(outs), grid_spec=pltpu.PrefetchSca...  7.02 us
  transfers between devices with their start and end apart: 36, of which 22 were waited for; matrix products, arithmetic and copies ran while one was open for 4% of the time, Pallas kernels for 7%

profile of v3, /device:TPU:0, one launch (start us, length us, event | category | flops | bytes accessed | tf_op | source)
XLA Modules:
  0.0 331.3 jit_solution(5474939297760003270)
XLA Ops:
  7.2 1.4 slice_bitcast_fusion
  9.1 2.6 collective-permute-start.1
  11.7 1.5 collective-permute-start.6
  16.6 1.9 copy-done.4
  18.5 3.5 %shard_map.59 = (f32[2560,128]{1,0:T(8,128)S(1)}, bf16[1280,1024]{1,0:T(8,128)(2,1)S(1)}) custom-call(s32[25]{0:T(128)S(1)} %pad_add_fusion.info_ref, bf16[1,3072,512]{2,1,0:T(8,128)(2,1)S(1)} %copy-done.4, bf16[1280,512]{1,0:T(8,128)(2,1)S(1)} %collective-permute-done.other_ref), custom_call_target="tpu_custom_call" | custom-call | flops 1342177280 | bytes 16777216 | tf_op jit(solution)/shard_map/pallas_call | solution.py:234
  22.2 1.6 collective-permute-start.7
  23.8 1.4 collective-permute-start.2
  25.2 3.5 %shard_map.60 = (f32[1024,256]{1,0:T(8,128)S(1)}, f32[1024,256]{1,0:T(8,128)S(1)}, f32[1024,256]{1,0:T(8,128)S(1)}, f32[1024,256]{1,0:T(8,128)S(1)}) custom-call(s32[25]{0:T(128)S(1)} %pad_add_fusion.info_ref, bf16[1280,1024]{1,0:T(8,128)(2,1)S(1)} %get-tuple-element.14.a_ref, bf16[1,3072,1024]{2,1,0:T(8,128)(2,1)S(1)} %copy-done.5), custom_call_target="tpu_custom_call" | custom-call | flops 2684354560 | bytes 16777216 | tf_op jit(solution)/shard_map/pallas_call | solution.py:234
  30.1 1.4 collective-permute-start.12
  32.8 1.6 collective-permute-start.16
  34.5 1.4 collective-permute-start.8
  36.0 8.1 %collective-permute-done.24 = f32[2,2,2,64,256]{4,3,2,1,0:T(8,128)S(1)} collective-permute-done((f32[2,2,2,64,256]{4,3,2,1,0:T(8,128)S(1)}, f32[2,2,2,64,256]{4,3,2,1,0:T(8,128)S(1)}, u32[]{:S(2)}, u32[]{:S(2)}) %collective-permute-start.24) | collective-permute-done | bytes 524320 | tf_op jit(solution)/shard_map/ppermute | solution.py:327
  44.1 1.6 collective-permute-start.3
  46.7 1.3 collective-permute-start.25
  49.1 7.7 %collective-permute-done.12 = f32[2,2,2,64,256]{4,3,2,1,0:T(8,128)S(1)} collective-permute-done((f32[2,2,2,64,256]{4,3,2,1,0:T(8,128)S(1)}, f32[2,2,2,64,256]{4,3,2,1,0:T(8,128)S(1)}, u32[]{:S(2)}, u32[]{:S(2)}) %collective-permute-start.12) | collective-permute-done | bytes 524320 | tf_op jit(solution)/shard_map/ppermute | solution.py:327
  57.6 6.2 %collective-permute-done.8 = f32[2,2,2,80,128]{4,3,2,1,0:T(8,128)S(1)} collective-permute-done((f32[2,2,2,80,128]{4,3,2,1,0:T(8,128)S(1)}, f32[2,2,2,80,128]{4,3,2,1,0:T(8,128)S(1)}, u32[]{:S(2)}, u32[]{:S(2)}) %collective-permute-start.8) | collective-permute-done | bytes 327712 | tf_op jit(solution)/shard_map/ppermute | solution.py:327
  63.9 1.6 collective-permute-start.9
  66.2 4.0 %collective-permute-done.9 = f32[2,2,80,128]{3,2,0,1:T(8,128)S(1)} collective-permute-done((f32[2,2,80,128]{3,2,0,1:T(8,128)S(1)}, f32[2,2,80,128]{3,2,0,1:T(8,128)S(1)}, u32[]{:S(2)}, u32[]{:S(2)}) %collective-permute-start.9) | collective-permute-done | bytes 163872 | tf_op jit(solution)/shard_map/ppermute | solution.py:327
  70.2 2.5 collective-permute-start.10
  72.9 2.4 collective-permute-start.5
  75.7 2.6 collective-permute-done.5
  83.5 1.9 collective-permute-start.26
  86.8 8.0 %collective-permute-done.13 = f32[2,2,2,64,256]{4,3,1,0,2:T(8,128)} collective-permute-done((f32[2,2,2,64,256]{4,3,1,0,2:T(8,128)}, f32[2,2,2,64,256]{4,3,1,0,2:T(8,128)}, u32[]{:S(2)}, u32[]{:S(2)}) %collective-permute-start.13) | collective-permute-done | bytes 524320 | tf_op jit(solution)/shard_map/ppermute | solution.py:327
  95.9 2.0 collective-permute-start.14
  98.1 1.3 collective-permute-start.18
  99.5 3.4 %collective-permute-start.27 = (f32[2,64,256]{2,1,0:T(8,128)S(1)}, f32[2,64,256]{2,1,0:T(8,128)S(1)}, u32[]{:S(2)}, u32[]{:S(2)}) collective-permute-start(f32[2,64,256]{2,1,0:T(8,128)S(1)} %dynamic-slice_bitcast_fusion.11), channel_id=1, source_target_pairs={{0,16},{2,18},{4,20},{6,22},{8,24},{10,26},{12,28},{14,30},{16,0},... | collective-permute-start | bytes 393224 | tf_op jit(solution)/shard_map/ppermute | solution.py:327
  102.9 1.4 collective-permute-start.23
  104.3 8.8 %collective-permute-done.14 = f32[2,2,64,256]{3,2,1,0:T(8,128)S(1)} collective-permute-done((f32[2,2,64,256]{3,2,1,0:T(8,128)S(1)}, f32[2,2,64,256]{3,2,1,0:T(8,128)S(1)}, u32[]{:S(2)}, u32[]{:S(2)}) %collective-permute-start.14) | collective-permute-done | bytes 262176 | tf_op jit(solution)/shard_map/ppermute | solution.py:327
  113.2 1.3 collective-permute-start.15
  114.5 5.4 %collective-permute-done.18 = f32[2,2,64,256]{3,2,1,0:T(8,128)S(1)} collective-permute-done((f32[2,2,64,256]{3,2,1,0:T(8,128)S(1)}, f32[2,2,64,256]{3,2,1,0:T(8,128)S(1)}, u32[]{:S(2)}, u32[]{:S(2)}) %collective-permute-start.18) | collective-permute-done | bytes 262176 | tf_op jit(solution)/shard_map/ppermute | solution.py:327
  120.0 3.0 collective-permute-start.19
  123.1 11.1 %collective-permute-done.15 = f32[2,64,256]{2,1,0:T(8,128)S(1)} collective-permute-done((f32[2,64,256]{2,1,0:T(8,128)S(1)}, f32[2,64,256]{2,1,0:T(8,128)S(1)}, u32[]{:S(2)}, u32[]{:S(2)}) %collective-permute-start.15) | collective-permute-done | bytes 131104 | tf_op jit(solution)/shard_map/ppermute | solution.py:327
  134.2 3.9 %collective-permute-done.19 = f32[2,64,256]{2,1,0:T(8,128)S(1)} collective-permute-done((f32[2,64,256]{2,1,0:T(8,128)S(1)}, f32[2,64,256]{2,1,0:T(8,128)S(1)}, u32[]{:S(2)}, u32[]{:S(2)}) %collective-permute-start.19) | collective-permute-done | bytes 131104 | tf_op jit(solution)/shard_map/ppermute | solution.py:327
  138.3 1.5 collective-permute-done.28
  140.0 22.7 %all-gather.9.cloned.1.call-done = f32[32,160,128]{2,1,0:T(8,128)} async-done(((f32[2,160,128]{2,1,0:T(8,128)}), f32[32,160,128]{2,1,0:T(8,128)}) %all-gather.9.cloned.1.call-update) | async-done | bytes 2621456 | tf_op jit(solution)/shard_map/all_gather | solution.py:382
  162.7 1.7 copy-done.6
  164.4 29.5 %shard_map.61 = (f32[512,1024]{1,0:T(8,128)S(1)}, s32[264,128]{1,0:T(8,128)S(1)}, f32[512,640]{1,0:T(8,128)S(1)}) custom-call(f32[16,2,160,128]{3,2,1,0:T(8,128)S(1)} %bitcast.363, f32[128,1024]{1,0:T(8,128)S(1)} %bitcast.362), custom_call_target="tpu_custom_call" | custom-call | flops 16106127360 | bytes 2097152 | tf_op jit(solution)/shard_map/pallas_call | solution.py:178
  197.3 1.3 copy-done.8
  198.6 16.6 %shard_map.62 = (f32[512,1024]{1,0:T(8,128)S(1)}, s32[264,128]{1,0:T(8,128)S(1)}) custom-call(f32[512,640]{1,0:T(8,128)S(1)} %copy-done.8), custom_call_target="tpu_custom_call" | custom-call | flops 16106127360 | bytes 2097152 | tf_op jit(solution)/shard_map/pallas_call | solution.py:178
  215.2 1.3 copy-done.2
  222.4 1.4 collective-permute-done.30
  224.2 2.5 maximum_maximum_fusion
  226.6 31.1 %all-gather.7.cloned.1.call-done.q_ref.s_ref = s32[16,264,128]{2,1,0:T(8,128)} async-done(((s32[1,264,128]{2,1,0:T(8,128)}), s32[16,264,128]{2,1,0:T(8,128)}) %all-gather.7.cloned.1.call-update) | async-done | bytes 2162704 | tf_op jit(solution)/shard_map/all_gather | solution.py:396
  257.7 1.6 copy-done.1
  259.3 2.8 shard_map.63.rest_0_
  262.1 58.0 %all-gather.5.cloned.1.call-done.q_ref.s_ref = s32[16,264,128]{2,1,0:T(8,128)} async-done(((s32[1,264,128]{2,1,0:T(8,128)}), s32[16,264,128]{2,1,0:T(8,128)}) %all-gather.5.cloned.1.call-update) | async-done | bytes 2162704 | tf_op jit(solution)/shard_map/all_gather | solution.py:396
  320.1 1.6 copy-done
  321.7 2.8 shard_map.64
  (130 shorter events, 25.9 us)
Async XLA Ops:
  7.2 6.8 %copy-start.9 = (s32[1,24]{1,0:T(1,128)S(1)}, s32[1,24]{1,0:T(1,128)}, u32[]{:S(2)}) copy-start(s32[1,24]{1,0:T(1,128)} %param.6) | copy-start | bytes 292
  7.2 155.5 %all-gather.9.cloned.1.call-start = ((), (), s32[]{:S(2)}) async-start(), calls=%async_computation.2 | async-start | bytes 2785280 | tf_op jit(solution)/shard_map/all_gather | solution.py:382
  8.6 8.0 %collective-permute-start = (bf16[1280,512]{1,0:T(8,128)(2,1)S(1)}, bf16[1280,512]{1,0:T(8,128)(2,1)S(1)}, u32[]{:S(2)}, u32[]{:S(2)}) collective-permute-start(bf16[1280,512]{1,0:T(8,128)(2,1)S(1)} %slice_bitcast_fusion), channel_id=1, source_target_pairs={{0,1},{1,0},{2,3},{3,2},{4,5},{5,4},{6,7},{7,6},{8,9},{9,8},{10,11... | collective-permute-start | bytes 3932168 | tf_op jit(solution)/shard_map/ppermute | solution.py:370
  9.1 4.9 %collective-permute-start.1 = (s32[1]{0:T(128)}, s32[1]{0:T(128)}, u32[]{:S(2)}, u32[]{:S(2)}) collective-permute-start(s32[1]{0:T(128)} %param.7), channel_id=1, source_target_pairs={{0,2},{2,0},{4,6},{6,4},{8,10},{10,8},{12,14},{14,12},{16,18},{18,... | collective-permute-start | bytes 20 | tf_op jit(solution)/shard_map/ppermute | solution.py:327
  11.7 3.6 %collective-permute-start.6 = (s32[1]{0:T(128)}, s32[1]{0:T(128)}, u32[]{:S(2)}, u32[]{:S(2)}) collective-permute-start(s32[1]{0:T(128)} %param.7), channel_id=1, source_target_pairs={{0,4},{2,6},{4,0},{6,2},{8,12},{10,14},{12,8},{14,10},{16,20},{18,... | collective-permute-start | bytes 20 | tf_op jit(solution)/shard_map/ppermute | solution.py:327
  16.6 1.9 copy-start.4
  18.5 6.7 %copy-start.5 = (bf16[1,3072,1024]{2,1,0:T(8,128)(2,1)S(1)}, bf16[1,3072,1024]{2,1,0:T(8,128)(2,1)}, u32[]{:S(2)}) copy-start(bf16[1,3072,1024]{2,1,0:T(8,128)(2,1)} %trail_ref.1) | copy-start | bytes 18874372
  22.2 10.7 %collective-permute-start.7 = (f32[2,2,2,80,128]{4,3,2,1,0:T(8,128)S(1)}, f32[2,2,2,80,128]{4,3,2,1,0:T(8,128)S(1)}, u32[]{:S(2)}, u32[]{:S(2)}) collective-permute-start(f32[2,2,2,80,128]{4,3,2,1,0:T(8,128)S(1)} %dynamic-slice_bitcast_fusion.4), channel_id=1, source_target_pairs={{0,4},{2,6},{4,0},{6,2},{8,12},{10,14},{12,8},{14,10},{16,20},{18,... | collective-permute-start | bytes 983048 | tf_op jit(solution)/shard_map/ppermute | solution.py:327
  23.8 10.7 %collective-permute-start.2 = (f32[2,2,2,80,128]{4,3,2,1,0:T(8,128)S(1)}, f32[2,2,2,80,128]{4,3,2,1,0:T(8,128)S(1)}, u32[]{:S(2)}, u32[]{:S(2)}) collective-permute-start(f32[2,2,2,80,128]{4,3,2,1,0:T(8,128)S(1)} %dynamic-slice_bitcast_fusion.5), channel_id=1, source_target_pairs={{0,2},{2,0},{4,6},{6,4},{8,10},{10,8},{12,14},{14,12},{16,18},{18,... | collective-permute-start | bytes 983048 | tf_op jit(solution)/shard_map/ppermute | solution.py:327
  28.7 15.4 %collective-permute-start.24 = (f32[2,2,2,64,256]{4,3,2,1,0:T(8,128)S(1)}, f32[2,2,2,64,256]{4,3,2,1,0:T(8,128)S(1)}, u32[]{:S(2)}, u32[]{:S(2)}) collective-permute-start(f32[2,2,2,64,256]{4,3,2,1,0:T(8,128)S(1)} %dynamic-slice_bitcast_fusion), channel_id=1, source_target_pairs={{0,4},{2,6},{4,0},{6,2},{8,12},{10,14},{12,8},{14,10},{16,20},{18,... | collective-permute-start | bytes 1572872 | tf_op jit(solution)/shard_map/ppermute | solution.py:327
  29.3 17.4 %collective-permute-start.20 = (f32[2,2,2,64,256]{4,3,2,1,0:T(8,128)S(1)}, f32[2,2,2,64,256]{4,3,2,1,0:T(8,128)S(1)}, u32[]{:S(2)}, u32[]{:S(2)}) collective-permute-start(f32[2,2,2,64,256]{4,3,2,1,0:T(8,128)S(1)} %dynamic-slice_bitcast_fusion.1), channel_id=1, source_target_pairs={{0,2},{2,0},{4,6},{6,4},{8,10},{10,8},{12,14},{14,12},{16,18},{18,... | collective-permute-start | bytes 1572872 | tf_op jit(solution)/shard_map/ppermute | solution.py:327
  30.1 26.7 %collective-permute-start.12 = (f32[2,2,2,64,256]{4,3,2,1,0:T(8,128)S(1)}, f32[2,2,2,64,256]{4,3,2,1,0:T(8,128)S(1)}, u32[]{:S(2)}, u32[]{:S(2)}) collective-permute-start(f32[2,2,2,64,256]{4,3,2,1,0:T(8,128)S(1)} %dynamic-slice_bitcast_fusion.3), channel_id=1, source_target_pairs={{0,2},{2,0},{4,6},{6,4},{8,10},{10,8},{12,14},{14,12},{16,18},{18,... | collective-permute-start | bytes 1572872 | tf_op jit(solution)/shard_map/ppermute | solution.py:327
  32.8 48.2 %collective-permute-start.16 = (f32[2,2,2,64,256]{4,3,2,1,0:T(8,128)}, f32[2,2,2,64,256]{4,3,2,1,0:T(8,128)}, u32[]{:S(2)}, u32[]{:S(2)}) collective-permute-start(f32[2,2,2,64,256]{4,3,2,1,0:T(8,128)} %dynamic-slice_bitcast_fusion.2), channel_id=1, source_target_pairs={{0,4},{2,6},{4,0},{6,2},{8,12},{10,14},{12,8},{14,10},{16,20},{18,... | collective-permute-start | bytes 1572872 | tf_op jit(solution)/shard_map/ppermute | solution.py:327
  34.5 29.3 %collective-permute-start.8 = (f32[2,2,2,80,128]{4,3,2,1,0:T(8,128)S(1)}, f32[2,2,2,80,128]{4,3,2,1,0:T(8,128)S(1)}, u32[]{:S(2)}, u32[]{:S(2)}) collective-permute-start(f32[2,2,2,80,128]{4,3,2,1,0:T(8,128)S(1)} %fusion.37), channel_id=1, source_target_pairs={{0,2},{2,0},{4,6},{6,4},{8,10},{10,8},{12,14},{14,12},{16,18},{18,... | collective-permute-start | bytes 983048 | tf_op jit(solution)/shard_map/ppermute | solution.py:327
  44.1 21.5 %collective-permute-start.3 = (f32[2,2,2,80,128]{4,3,2,1,0:T(8,128)S(1)}, f32[2,2,2,80,128]{4,3,2,1,0:T(8,128)S(1)}, u32[]{:S(2)}, u32[]{:S(2)}) collective-permute-start(f32[2,2,2,80,128]{4,3,2,1,0:T(8,128)S(1)} %fusion.42), channel_id=1, source_target_pairs={{0,4},{2,6},{4,0},{6,2},{8,12},{10,14},{12,8},{14,10},{16,20},{18,... | collective-permute-start | bytes 983048 | tf_op jit(solution)/shard_map/ppermute | solution.py:327
  46.7 36.7 %collective-permute-start.25 = (f32[2,2,2,64,256]{4,3,1,0,2:T(8,128)}, f32[2,2,2,64,256]{4,3,1,0,2:T(8,128)S(1)}, u32[]{:S(2)}, u32[]{:S(2)}) collective-permute-start(f32[2,2,2,64,256]{4,3,1,0,2:T(8,128)} %bitcast.347), channel_id=1, source_target_pairs={{0,2},{2,0},{4,6},{6,4},{8,10},{10,8},{12,14},{14,12},{16,18},{18,... | collective-permute-start | bytes 1572872 | tf_op jit(solution)/shard_map/ppermute | solution.py:327
  56.8 28.6 %collective-permute-start.21 = (f32[2,2,2,64,256]{4,3,1,0,2:T(8,128)}, f32[2,2,2,64,256]{4,3,1,0,2:T(8,128)}, u32[]{:S(2)}, u32[]{:S(2)}) collective-permute-start(f32[2,2,2,64,256]{4,3,1,0,2:T(8,128)} %bitcast.348), channel_id=1, source_target_pairs={{0,4},{2,6},{4,0},{6,2},{8,12},{10,14},{12,8},{14,10},{16,20},{18,... | collective-permute-start | bytes 1572872 | tf_op jit(solution)/shard_map/ppermute | solution.py:327
  63.9 6.3 %collective-permute-start.9 = (f32[2,2,80,128]{3,2,0,1:T(8,128)S(1)}, f32[2,2,80,128]{3,2,0,1:T(8,128)S(1)}, u32[]{:S(2)}, u32[]{:S(2)}) collective-permute-start(f32[2,2,80,128]{3,2,0,1:T(8,128)S(1)} %bitcast.370), channel_id=1, source_target_pairs={{0,8},{2,10},{4,12},{6,14},{8,0},{10,2},{12,4},{14,6},{16,24},{18,... | collective-permute-start | bytes 491528 | tf_op jit(solution)/shard_map/ppermute | solution.py:327
  65.7 7.1 %collective-permute-start.4 = (f32[2,2,80,128]{3,2,0,1:T(8,128)S(1)}, f32[2,2,80,128]{3,2,0,1:T(8,128)S(1)}, u32[]{:S(2)}, u32[]{:S(2)}) collective-permute-start(f32[2,2,80,128]{3,2,0,1:T(8,128)S(1)} %bitcast.371), channel_id=1, source_target_pairs={{0,8},{2,10},{4,12},{6,14},{8,0},{10,2},{12,4},{14,6},{16,24},{18,... | collective-permute-start | bytes 491528 | tf_op jit(solution)/shard_map/ppermute | solution.py:327
  70.2 5.4 %collective-permute-start.10 = (f32[2,80,128]{2,1,0:T(8,128)S(1)}, f32[2,80,128]{2,1,0:T(8,128)S(1)}, u32[]{:S(2)}, u32[]{:S(2)}) collective-permute-start(f32[2,80,128]{2,1,0:T(8,128)S(1)} %dynamic-slice_bitcast_fusion.15), channel_id=1, source_target_pairs={{0,16},{2,18},{4,20},{6,22},{8,24},{10,26},{12,28},{14,30},{16,0},... | collective-permute-start | bytes 245768 | tf_op jit(solution)/shard_map/ppermute | solution.py:327
  72.9 5.4 %collective-permute-start.5 = (f32[2,80,128]{2,1,0:T(8,128)S(1)}, f32[2,80,128]{2,1,0:T(8,128)S(1)}, u32[]{:S(2)}, u32[]{:S(2)}) collective-permute-start(f32[2,80,128]{2,1,0:T(8,128)S(1)} %dynamic-slice_bitcast_fusion.16), channel_id=1, source_target_pairs={{0,16},{2,18},{4,20},{6,22},{8,24},{10,26},{12,28},{14,30},{16,0},... | collective-permute-start | bytes 245768 | tf_op jit(solution)/shard_map/ppermute | solution.py:327
  78.3 1.7 collective-permute-start.11
  79.3 15.5 %collective-permute-start.13 = (f32[2,2,2,64,256]{4,3,1,0,2:T(8,128)}, f32[2,2,2,64,256]{4,3,1,0,2:T(8,128)}, u32[]{:S(2)}, u32[]{:S(2)}) collective-permute-start(f32[2,2,2,64,256]{4,3,1,0,2:T(8,128)} %bitcast.350), channel_id=1, source_target_pairs={{0,4},{2,6},{4,0},{6,2},{8,12},{10,14},{12,8},{14,10},{16,20},{18,... | collective-permute-start | bytes 1572872 | tf_op jit(solution)/shard_map/ppermute | solution.py:327
  80.8 176.9 %all-gather.7.cloned.1.call-start = ((), (), s32[]{:S(2)}) async-start(), calls=%async_computation.1 | async-start | bytes 2297856 | tf_op jit(solution)/shard_map/all_gather | solution.py:396
  82.4 15.5 %collective-permute-start.17 = (f32[2,2,2,64,256]{4,3,1,0,2:T(8,128)S(1)}, f32[2,2,2,64,256]{4,3,1,0,2:T(8,128)S(1)}, u32[]{:S(2)}, u32[]{:S(2)}) collective-permute-start(f32[2,2,2,64,256]{4,3,1,0,2:T(8,128)S(1)} %bitcast.369), channel_id=1, source_target_pairs={{0,2},{2,0},{4,6},{6,4},{8,10},{10,8},{12,14},{14,12},{16,18},{18,... | collective-permute-start | bytes 1572872 | tf_op jit(solution)/shard_map/ppermute | solution.py:327
  83.5 15.9 %collective-permute-start.26 = (f32[2,2,64,256]{3,2,1,0:T(8,128)S(1)}, f32[2,2,64,256]{3,2,1,0:T(8,128)S(1)}, u32[]{:S(2)}, u32[]{:S(2)}) collective-permute-start(f32[2,2,64,256]{3,2,1,0:T(8,128)S(1)} %dynamic-slice_bitcast_fusion.7), channel_id=1, source_target_pairs={{0,8},{2,10},{4,12},{6,14},{8,0},{10,2},{12,4},{14,6},{16,24},{18,... | collective-permute-start | bytes 786440 | tf_op jit(solution)/shard_map/ppermute | solution.py:327
  86.5 16.3 %collective-permute-start.22 = (f32[2,2,64,256]{3,2,1,0:T(8,128)S(1)}, f32[2,2,64,256]{3,2,1,0:T(8,128)S(1)}, u32[]{:S(2)}, u32[]{:S(2)}) collective-permute-start(f32[2,2,64,256]{3,2,1,0:T(8,128)S(1)} %dynamic-slice_bitcast_fusion.8), channel_id=1, source_target_pairs={{0,8},{2,10},{4,12},{6,14},{8,0},{10,2},{12,4},{14,6},{16,24},{18,... | collective-permute-start | bytes 786440 | tf_op jit(solution)/shard_map/ppermute | solution.py:327
  95.9 17.2 %collective-permute-start.14 = (f32[2,2,64,256]{3,2,1,0:T(8,128)S(1)}, f32[2,2,64,256]{3,2,1,0:T(8,128)S(1)}, u32[]{:S(2)}, u32[]{:S(2)}) collective-permute-start(f32[2,2,64,256]{3,2,1,0:T(8,128)S(1)} %dynamic-slice_bitcast_fusion.10), channel_id=1, source_target_pairs={{0,8},{2,10},{4,12},{6,14},{8,0},{10,2},{12,4},{14,6},{16,24},{18,... | collective-permute-start | bytes 786440 | tf_op jit(solution)/shard_map/ppermute | solution.py:327
  98.1 21.9 %collective-permute-start.18 = (f32[2,2,64,256]{3,2,1,0:T(8,128)S(1)}, f32[2,2,64,256]{3,2,1,0:T(8,128)S(1)}, u32[]{:S(2)}, u32[]{:S(2)}) collective-permute-start(f32[2,2,64,256]{3,2,1,0:T(8,128)S(1)} %dynamic-slice_bitcast_fusion.9), channel_id=1, source_target_pairs={{0,8},{2,10},{4,12},{6,14},{8,0},{10,2},{12,4},{14,6},{16,24},{18,... | collective-permute-start | bytes 786440 | tf_op jit(solution)/shard_map/ppermute | solution.py:327
  99.5 23.6 %collective-permute-start.27 = (f32[2,64,256]{2,1,0:T(8,128)S(1)}, f32[2,64,256]{2,1,0:T(8,128)S(1)}, u32[]{:S(2)}, u32[]{:S(2)}) collective-permute-start(f32[2,64,256]{2,1,0:T(8,128)S(1)} %dynamic-slice_bitcast_fusion.11), channel_id=1, source_target_pairs={{0,16},{2,18},{4,20},{6,22},{8,24},{10,26},{12,28},{14,30},{16,0},... | collective-permute-start | bytes 393224 | tf_op jit(solution)/shard_map/ppermute | solution.py:327
  102.9 20.1 %collective-permute-start.23 = (f32[2,64,256]{2,1,0:T(8,128)S(1)}, f32[2,64,256]{2,1,0:T(8,128)S(1)}, u32[]{:S(2)}, u32[]{:S(2)}) collective-permute-start(f32[2,64,256]{2,1,0:T(8,128)S(1)} %dynamic-slice_bitcast_fusion.12), channel_id=1, source_target_pairs={{0,16},{2,18},{4,20},{6,22},{8,24},{10,26},{12,28},{14,30},{16,0},... | collective-permute-start | bytes 393224 | tf_op jit(solution)/shard_map/ppermute | solution.py:327
  113.2 21.0 %collective-permute-start.15 = (f32[2,64,256]{2,1,0:T(8,128)S(1)}, f32[2,64,256]{2,1,0:T(8,128)S(1)}, u32[]{:S(2)}, u32[]{:S(2)}) collective-permute-start(f32[2,64,256]{2,1,0:T(8,128)S(1)} %dynamic-slice_bitcast_fusion.14), channel_id=1, source_target_pairs={{0,16},{2,18},{4,20},{6,22},{8,24},{10,26},{12,28},{14,30},{16,0},... | collective-permute-start | bytes 393224 | tf_op jit(solution)/shard_map/ppermute | solution.py:327
  120.0 18.2 %collective-permute-start.19 = (f32[2,64,256]{2,1,0:T(8,128)S(1)}, f32[2,64,256]{2,1,0:T(8,128)S(1)}, u32[]{:S(2)}, u32[]{:S(2)}) collective-permute-start(f32[2,64,256]{2,1,0:T(8,128)S(1)} %dynamic-slice_bitcast_fusion.13), channel_id=1, source_target_pairs={{0,16},{2,18},{4,20},{6,22},{8,24},{10,26},{12,28},{14,30},{16,0},... | collective-permute-start | bytes 393224 | tf_op jit(solution)/shard_map/ppermute | solution.py:327
  138.3 1.6 collective-permute-start.28
  162.7 1.7 copy-start.6
  193.9 1.1 copy-start.7
  195.0 1.4 collective-permute-start.32
  197.2 122.9 %all-gather.5.cloned.1.call-start = ((), (), s32[]{:S(2)}) async-start(), calls=%async_computation | async-start | bytes 2297856 | tf_op jit(solution)/shard_map/all_gather | solution.py:396
  197.3 1.3 copy-start.8
  215.2 1.3 copy-start.2
  216.5 1.4 collective-permute-start.31
  219.0 1.6 copy-start.3
  219.3 2.7 collective-permute-start.29
  221.1 2.7 collective-permute-start.30
  257.7 1.6 copy-start.1
  320.1 1.6 copy-start
Sparse Core Ops, SparseCore 0:
  80.9 81.7 all-gather.8
  197.4 60.2 all-gather.6
  260.5 59.6 all-gather.4
